TPU v7x, 32 devices: a whole 2x2x4 slice. The times are simulated.
32 devices in a mesh: sx: 2 (over y), sy: 4 (over x, core), sz: 4 (over z).
Axes of the slice: x: 2, y: 2, z: 4, core: 2. Of those that a mesh axis runs over, the one named last changes fastest.
Arguments:
- right_side: bfloat16 [2, 4, 4, 1536, 256], P('sx', 'sy', 'sz'), may hold values from -6 to 6
- interface_inverse: bfloat16 [2, 4, 4, 1536, 1536], P('sx', 'sy', 'sz'), may hold values from -2 to 2, as said below
- face_link: int32 [2, 4, 4, 4], P('sx', 'sy', 'sz'), may hold values 0 or 1
- far_target: int32 [2, 4, 4, 8, 1], P('sx', 'sy', 'sz'), may hold values from 0 to 7; in each aligned block of 8 rows (0 to 7, 8 to 15, ..., all dimensions but the last counted through in order) at most 3 rows name the same one
- far_rank: int32 [2, 4, 4, 8], P('sx', 'sy', 'sz'), may hold values from 1 to 16
- far_basis: bfloat16 [2, 4, 4, 8, 16, 1536], P('sx', 'sy', 'sz'), may hold values from -0.15625 to 0.15625
- patch_basis: bfloat16 [2, 4, 4, 16, 1536], P('sx', 'sy', 'sz'), may hold values from -0.5 to 0.5
- corner_basis: bfloat16 [2, 4, 4, 8, 1536], P('sx', 'sy', 'sz'), may hold values from -1 to 1
- corner_row: int32 [2, 4, 4, 8], P('sx', 'sy', 'sz'), may hold values from 0 to 255
- coarse_inverse: bfloat16 [256, 256], P('sy'), may hold values from -2 to 2, as said below
Outputs:
- multipliers: float32 [2, 4, 4, 1536, 256], P('sx', 'sy', 'sz')
- interface_field: bfloat16 [2, 4, 4, 1536, 256], P('sx', 'sy', 'sz')
Inputs may be any that keep to these rules, and one draw needn't show every extreme that they name: `far_target`: within one subdomain's 8 entries no target is named more than 3 times, a bound that some block reaches. `interface_inverse`: each subdomain's block is a dense matrix with a positive diagonal that exceeds its row's off-diagonal magnitude in the root-mean-square sense. `coarse_inverse`: A dense matrix with a positive diagonal that exceeds its row's off-diagonal magnitude in the root-mean-square sense.
All inputs are finite; a program needn't handle non-finite values. No bound on the sum of `face_link` on one device may be relied on, other than what follows from the above.
Results may differ from a plain program's by a relative error of at most 0.0085.
Values may be sent and summed in bfloat16 or wider, within the bound.
A program may use at most 64 MiB of HBM per device.

v0:
```python
import jax
import jax.numpy as jnp
from jax import lax
from jax.sharding import PartitionSpec as P

MOST = 3
ITERS = 2


def shifted(block, axis, distance):
    devices = range(lax.axis_size(axis))
    route = [(i - distance, i) for i in devices if i - distance in devices]
    return lax.ppermute(block, axis, route)


def neighbour_faces(solved, face_rows, link_weights, padding):
    pieces = []
    for offset, sent_face in ((1, 1), (-1, 0)):
        outgoing = solved[sent_face * face_rows : (sent_face + 1) * face_rows]
        pieces.append(shifted(outgoing, "sx", offset))
    for offset, sent_face in ((1, 3), (-1, 2)):
        outgoing = solved[sent_face * face_rows : (sent_face + 1) * face_rows]
        pieces.append(shifted(outgoing, "sy", offset))
    scaled = [pieces[number].astype(jnp.float32) * link_weights[number] for number in range(4)]
    return jnp.concatenate(scaled + [padding], axis=0)


def body(
    right_side,
    interface_inverse,
    face_link,
    far_target,
    far_rank,
    far_basis,
    patch_basis,
    corner_basis,
    corner_row,
    coarse_inverse,
):
    order_size = interface_inverse.shape[-1]
    columns = right_side.shape[-1]
    face_rows = order_size // 6
    inverse = interface_inverse.reshape(order_size, order_size)
    source = right_side.reshape(order_size, columns).astype(jnp.float32)
    link_weights = face_link.reshape(4).astype(jnp.float32)
    targets = far_target.reshape(-1)
    entries = targets.shape[0]
    rank_limit = far_basis.shape[-2]
    bases = far_basis.reshape(entries * rank_limit, order_size)
    kept_rows = (
        jnp.arange(rank_limit, dtype=jnp.int32)[None, :] < far_rank.reshape(entries, 1)
    ).astype(jnp.float32)
    patch = patch_basis.reshape(rank_limit, order_size)
    corners = corner_basis.reshape(-1, order_size)
    corner_ids = corner_row.reshape(-1)
    coarse_order = coarse_inverse.shape[1]
    group_size = lax.axis_size("sx") * lax.axis_size("sz")
    corner_hot = (corner_ids[None, :] == jnp.arange(coarse_order, dtype=jnp.int32)[:, None]).astype(
        jnp.float32
    )
    pick_table = corner_hot.T.astype(jnp.bfloat16)
    padding = jnp.zeros((order_size - 4 * face_rows, columns), jnp.float32)
    earlier = (
        jnp.arange(entries, dtype=jnp.int32)[:, None]
        > jnp.arange(entries, dtype=jnp.int32)[None, :]
    )
    same_target = targets[:, None] == targets[None, :]
    slot_number = jnp.sum(jnp.logical_and(earlier, same_target).astype(jnp.int32), axis=1)
    slot_key = targets * MOST + slot_number
    route_table = (
        slot_key[None, :] == jnp.arange(group_size * MOST, dtype=jnp.int32)[:, None]
    ).astype(jnp.bfloat16)
    multipliers = source
    for sweep in range(ITERS):
        solved = jnp.dot(
            inverse, multipliers.astype(jnp.bfloat16), preferred_element_type=jnp.float32
        ).astype(jnp.bfloat16)
        neighbour = neighbour_faces(solved, face_rows, link_weights, padding)
        coefficient = jnp.dot(bases, solved, preferred_element_type=jnp.float32).reshape(
            entries, rank_limit, columns
        )
        coefficient = (
            (coefficient * kept_rows[:, :, None])
            .astype(jnp.bfloat16)
            .reshape(entries, rank_limit * columns)
        )
        routed = jnp.dot(route_table, coefficient, preferred_element_type=jnp.float32)
        outgoing = routed.astype(jnp.bfloat16).reshape(group_size, MOST, rank_limit, columns)
        arrived_slots = lax.all_to_all(
            outgoing, ("sx", "sz"), split_axis=0, concat_axis=0, tiled=True
        )
        arrived = jnp.sum(arrived_slots.astype(jnp.float32), axis=(0, 1))
        far_term = lax.dot_general(
            patch,
            arrived.astype(jnp.bfloat16),
            (((0,), (0,)), ((), ())),
            preferred_element_type=jnp.float32,
        )
        corner_terms = jnp.dot(corners, solved, preferred_element_type=jnp.float32)
        partial_sum = jnp.dot(corner_hot, corner_terms, precision=lax.Precision.HIGHEST)
        coarse_sum = lax.psum(partial_sum, ("sx", "sy", "sz")).astype(jnp.bfloat16)
        own_rows = jnp.dot(coarse_inverse, coarse_sum, preferred_element_type=jnp.float32).astype(
            jnp.bfloat16
        )
        coarse_field = lax.all_gather(own_rows, "sy", axis=0, tiled=True)
        picked = jnp.dot(pick_table, coarse_field, preferred_element_type=jnp.float32).astype(
            jnp.bfloat16
        )
        correction = lax.dot_general(
            corners, picked, (((0,), (0,)), ((), ())), preferred_element_type=jnp.float32
        )
        multipliers = (
            multipliers + source - (solved.astype(jnp.float32) - neighbour) - far_term - correction
        )
    interface_field = jnp.dot(
        inverse, multipliers.astype(jnp.bfloat16), preferred_element_type=jnp.float32
    ).astype(jnp.bfloat16)
    return (multipliers.reshape(right_side.shape), interface_field.reshape(right_side.shape))


def solution(mesh):
    return jax.shard_map(
        body,
        mesh=mesh,
        in_specs=(
            P("sx", "sy", "sz", None, None),
            P("sx", "sy", "sz", None, None),
            P("sx", "sy", "sz", None),
            P("sx", "sy", "sz", None, None),
            P("sx", "sy", "sz", None),
            P("sx", "sy", "sz", None, None, None),
            P("sx", "sy", "sz", None, None),
            P("sx", "sy", "sz", None, None),
            P("sx", "sy", "sz", None),
            P("sy", None),
        ),
        out_specs=(P("sx", "sy", "sz", None, None), P("sx", "sy", "sz", None, None)),
        check_vma=False,
    )
```

profile of v0, /device:TPU:0, one launch (start us, length us, event | category | flops | bytes accessed | tf_op | source)
XLA Modules:
  0.0 189.8 jit_solution(9723393189750765718)
XLA Ops:
  0.6 4.0 %fusion.10 = bf16[1536,256]{1,0:T(8,128)(2,1)S(1)} fusion(bf16[1,1,1,1536,1536]{4,3,2,1,0:T(8,128)(2,1)} %param.11, bf16[1,1,1,1536,256]{4,3,2,1,0:T(8,128)(2,1)} %param.10), kind=kOutput, calls=%fused_computation.16 | convolution fusion | flops 1208352768 | bytes 6291456 | tf_op jit(solution)/shard_map/dot_general | solution.py:75
  4.7 0.4 convolution_bitcast_fusion.5
  5.8 0.7 copy.47
  6.5 7.4 %all-to-all-start = ((bf16[8,3,16,256]{3,2,1,0:T(8,128)(2,1)}), bf16[8,3,16,256]{3,2,1,0:T(8,128)(2,1)}, u32[]{:S(2)}, u32[]{:S(2)}) async-start(bf16[8,3,16,256]{3,2,1,0:T(8,128)(2,1)} %bitcast.28), calls=%async_computation | async-start | bytes 393216 | tf_op jit(solution)/shard_map/all_to_all | solution.py:89
  14.0 0.8 fusion.52
  14.7 3.9 %collective-permute-start = (bf16[256,256]{1,0:T(8,128)(2,1)S(1)}, bf16[256,256]{1,0:T(8,128)(2,1)S(1)}, u32[]{:S(2)}, u32[]{:S(2)}) collective-permute-start(bf16[256,256]{1,0:T(8,128)(2,1)S(1)} %get-tuple-element.17), channel_id=1, source_target_pairs={{0,16},{1,17},{2,18},{3,19},{4,20},{5,21},{6,22},{7,23},{8,24},{9,... | collective-permute-start | bytes 393224 | tf_op jit(solution)/shard_map/ppermute | solution.py:13
  18.6 1.3 collective-permute-start.1
  19.9 2.0 %collective-permute-start.2 = (bf16[256,256]{1,0:T(8,128)(2,1)}, bf16[256,256]{1,0:T(8,128)(2,1)}, u32[]{:S(2)}, u32[]{:S(2)}) collective-permute-start(bf16[256,256]{1,0:T(8,128)(2,1)} %get-tuple-element.15), channel_id=1, source_target_pairs={{0,4},{4,8},{8,12},{1,5},{5,9},{9,13},{2,6},{6,10},{10,14},{3,7},{... | collective-permute-start | bytes 393224 | tf_op jit(solution)/shard_map/ppermute | solution.py:13
  21.9 1.3 collective-permute-start.3
  23.2 0.2 fusion.41
  23.4 0.3 fusion.32
  23.7 46.6 %all-reduce.2 = bf16[256,256]{1,0:T(8,128)(2,1)S(1)} all-reduce(f32[256,256]{1,0:T(8,128)S(1)} %fusion.32), channel_id=1, replica_groups=mesh['sx'=2,'sy'=4,'sz'=4] {'sx','sy','sz'}, use_global_device_ids=true, to_apply=%region_2.0 | all-reduce | flops 65536 | bytes 393216 | tf_op jit(solution)/shard_map/psum | solution.py:101
  70.5 5.9 %all_gather.6 = bf16[256,256]{1,0:T(8,128)(2,1)} all-gather(bf16[64,256]{1,0:T(8,128)(2,1)S(1)} %fusion.24), channel_id=1, replica_groups=mesh['sx'=2,'sy'=4,'sz'=4] {'sy'}, dimensions={0}, use_global_device_ids=true | all-gather | bytes 163840 | tf_op jit(solution)/shard_map/all_gather | solution.py:105
  76.4 0.7 fusion.53
  77.0 0.7 copy-done.6
  77.7 1.6 multiply_dynamic-update-slice_fusion.7
  79.3 1.6 multiply_dynamic-update-slice_fusion.6
  80.8 1.5 multiply_dynamic-update-slice_fusion.5
  82.4 1.6 multiply_dynamic-update-slice_fusion.4
  84.1 1.0 reduce_sum.34
  85.0 2.5 %fusion.9 = f32[1536,256]{1,0:T(8,128)} fusion(bf16[16,256]{1,0:T(8,128)(2,1)S(1)} %reduce_sum.34, f32[1536,256]{1,0:T(8,128)S(1)} %broadcast_dynamic-update-slice_fusion.1, bf16[1536,256]{1,0:T(8,128)(2,1)S(1)} %fusion.10, bf16[1,1,1,1536,256]{4,3,2,1,0:T(8,128)(2,1)S(1)} %copy-done.1, bf16[1,1,1,16,1536]{4,3,2,1,0:T(8,128)(2,1)} %param.16), kind=kOutput, calls=%fused_computation.15 | convolution fusion | flops 14942208 | bytes 4775936 | tf_op jit(solution)/shard_map/dot_general | solution.py:93
  87.5 2.0 %fusion.8 = f32[1536,256]{1,0:T(8,128)S(1)} fusion(f32[1536,256]{1,0:T(8,128)} %fusion.9, bf16[256,256]{1,0:T(8,128)(2,1)} %all_gather.6, bf16[1,1,1,8,1536]{4,3,2,1,0:T(8,128)(2,1)} %param.17, s32[8]{0:T(128)S(1)} %bitcast.107), kind=kOutput, calls=%fused_computation.13 | convolution fusion | flops 7741440 | bytes 3301408 | tf_op jit(solution)/shard_map/dot_general | solution.py:109
  89.6 3.7 %fusion.13 = bf16[256,1536]{0,1:T(8,128)(2,1)S(1)} fusion(bf16[1,1,1,1536,1536]{4,3,2,1,0:T(8,128)(2,1)} %param.11, f32[1536,256]{1,0:T(8,128)S(1)} %fusion.8), kind=kOutput, calls=%fused_computation.17 | convolution fusion | flops 1208745984 | bytes 7077888 | tf_op jit(solution)/shard_map/dot_general | solution.py:75
  93.3 1.1 convolution_bitcast_fusion.4
  94.6 1.7 copy.38
  96.2 1.6 reshape.101
  97.8 1.1 convolution_convert_fusion
  99.0 0.7 copy.48
  99.7 4.9 %all-to-all-start.1 = ((bf16[8,3,16,256]{3,2,1,0:T(8,128)(2,1)}), bf16[8,3,16,256]{3,2,1,0:T(8,128)(2,1)}, u32[]{:S(2)}, u32[]{:S(2)}) async-start(bf16[8,3,16,256]{3,2,1,0:T(8,128)(2,1)} %bitcast.103), calls=%async_computation.1 | async-start | bytes 393216 | tf_op jit(solution)/shard_map/all_to_all | solution.py:89
  104.6 0.8 fusion.51
  105.4 4.6 %collective-permute-start.4 = (bf16[256,256]{1,0:T(8,128)(2,1)}, bf16[256,256]{1,0:T(8,128)(2,1)}, u32[]{:S(2)}, u32[]{:S(2)}) collective-permute-start(bf16[256,256]{1,0:T(8,128)(2,1)} %get-tuple-element.13), channel_id=1, source_target_pairs={{0,16},{1,17},{2,18},{3,19},{4,20},{5,21},{6,22},{7,23},{8,24},{9,... | collective-permute-start | bytes 393224 | tf_op jit(solution)/shard_map/ppermute | solution.py:13
  109.9 1.3 collective-permute-start.5
  111.2 2.1 %collective-permute-start.6 = (bf16[256,256]{1,0:T(8,128)(2,1)}, bf16[256,256]{1,0:T(8,128)(2,1)}, u32[]{:S(2)}, u32[]{:S(2)}) collective-permute-start(bf16[256,256]{1,0:T(8,128)(2,1)} %get-tuple-element.11), channel_id=1, source_target_pairs={{0,4},{4,8},{8,12},{1,5},{5,9},{9,13},{2,6},{6,10},{10,14},{3,7},{... | collective-permute-start | bytes 393224 | tf_op jit(solution)/shard_map/ppermute | solution.py:13
  113.3 1.3 collective-permute-start.7
  114.6 0.9 fusion.31
  115.5 45.8 %all-reduce.3 = bf16[256,256]{1,0:T(8,128)(2,1)} all-reduce(f32[256,256]{1,0:T(8,128)} %fusion.31), channel_id=1, replica_groups=mesh['sx'=2,'sy'=4,'sz'=4] {'sx','sy','sz'}, use_global_device_ids=true, to_apply=%region_4.0 | all-reduce | flops 65536 | bytes 393216 | tf_op jit(solution)/shard_map/psum | solution.py:101
  161.3 1.1 fusion.25
  162.4 5.9 %all_gather.7 = bf16[256,256]{1,0:T(8,128)(2,1)} all-gather(bf16[64,256]{1,0:T(8,128)(2,1)S(1)} %fusion.25), channel_id=1, replica_groups=mesh['sx'=2,'sy'=4,'sz'=4] {'sy'}, dimensions={0}, use_global_device_ids=true | all-gather | bytes 163840 | tf_op jit(solution)/shard_map/all_gather | solution.py:105
  168.3 2.3 %multiply_dynamic-update-slice_fusion.3 = f32[1536,256]{1,0:T(8,128)} fusion(bf16[256,256]{1,0:T(8,128)(2,1)} %collective-permute-done.4, f32[]{:T(128)} %bitcast.2), kind=kLoop, calls=%fused_computation.38 | loop fusion | flops 131071 | bytes 393220
  170.5 2.3 %multiply_dynamic-update-slice_fusion.2 = f32[1536,256]{1,0:T(8,128)} fusion(f32[1536,256]{1,0:T(8,128)} %multiply_dynamic-update-slice_fusion.3, bf16[256,256]{1,0:T(8,128)(2,1)} %collective-permute-done.5, f32[]{:T(128)} %bitcast.3), kind=kLoop, calls=%fused_computation.37 | loop fusion | flops 131072 | bytes 393728
  172.8 2.2 %multiply_dynamic-update-slice_fusion.1 = f32[1536,256]{1,0:T(8,128)} fusion(f32[1536,256]{1,0:T(8,128)} %multiply_dynamic-update-slice_fusion.2, bf16[256,256]{1,0:T(8,128)(2,1)} %collective-permute-done.6, f32[]{:T(128)} %bitcast.4), kind=kLoop, calls=%fused_computation.36 | loop fusion | flops 131072 | bytes 393728
  175.0 2.3 %multiply_dynamic-update-slice_fusion = f32[1536,256]{1,0:T(8,128)} fusion(f32[1536,256]{1,0:T(8,128)} %multiply_dynamic-update-slice_fusion.1, bf16[256,256]{1,0:T(8,128)(2,1)} %collective-permute-done.7, f32[]{:T(128)} %bitcast.5), kind=kLoop, calls=%fused_computation.35 | loop fusion | flops 131072 | bytes 393728
  177.4 0.8 broadcast_dynamic-update-slice_fusion
  178.2 1.0 reduce_sum.35
  179.2 3.1 %fusion.7 = f32[1536,256]{1,0:T(8,128)} fusion(bf16[16,256]{1,0:T(8,128)(2,1)S(1)} %reduce_sum.35, f32[1536,256]{1,0:T(8,128)S(1)} %fusion.8, f32[1536,256]{1,0:T(8,128)} %broadcast_dynamic-update-slice_fusion, bf16[1,1,1,1536,256]{4,3,2,1,0:T(8,128)(2,1)S(1)} %copy-done.1, bf16[1,1,1,16,1536]{4,3,2,1,0:T(8,128)(2,1)} %param.16, ...), kind=kOutput, calls=%fused_computation.11 | convolution fusion | flops 14942208 | bytes 6348800 | tf_op jit(solution)/shard_map/dot_general | solution.py:93
  182.3 2.0 %fusion.6 = f32[1536,256]{1,0:T(8,128)S(1)} fusion(f32[1536,256]{1,0:T(8,128)} %fusion.7, bf16[256,256]{1,0:T(8,128)(2,1)} %all_gather.7, bf16[1,1,1,8,1536]{4,3,2,1,0:T(8,128)(2,1)} %param.17, s32[8]{0:T(128)S(1)} %bitcast.109), kind=kOutput, calls=%fused_computation.9 | convolution fusion | flops 7741440 | bytes 3301408 | tf_op jit(solution)/shard_map/dot_general | solution.py:109
  184.3 4.3 %fusion.19 = bf16[1,1,1,1536,256]{3,4,2,1,0:T(8,128)(2,1)S(1)} fusion(bf16[1,1,1,1536,1536]{4,3,2,1,0:T(8,128)(2,1)} %param.11, f32[1536,256]{1,0:T(8,128)S(1)} %fusion.6), kind=kOutput, calls=%fused_computation.19 | convolution fusion | flops 1208745984 | bytes 7077888 | tf_op jit(solution)/shard_map/dot_general | solution.py:115
  188.7 1.2 copy.41
  (44 shorter events, 1.1 us)
Async XLA Ops:
  0.6 4.0 %copy-start = (bf16[1,1,1,8,16,1536]{5,4,3,2,1,0:T(8,128)(2,1)S(1)}, bf16[1,1,1,8,16,1536]{5,4,3,2,1,0:T(8,128)(2,1)}, u32[]{:S(2)}) copy-start(bf16[1,1,1,8,16,1536]{5,4,3,2,1,0:T(8,128)(2,1)} %param.15) | copy-start | bytes 1179652
  4.6 0.7 copy-start.9
  4.7 0.7 copy-start.10
  5.1 18.1 %copy-start.4 = (bf16[1,1,1,8,1536]{4,3,2,1,0:T(8,128)(2,1)S(1)}, bf16[1,1,1,8,1536]{4,3,2,1,0:T(8,128)(2,1)}, u32[]{:S(2)}) copy-start(bf16[1,1,1,8,1536]{4,3,2,1,0:T(8,128)(2,1)} %param.17) | copy-start | bytes 73732
  5.6 17.8 %copy-start.3 = (f32[8,16,256]{2,0,1:T(8,128)}, f32[8,16,256]{2,0,1:T(8,128)S(1)}, u32[]{:S(2)}) copy-start(f32[8,16,256]{2,0,1:T(8,128)S(1)} %mul.74) | copy-start | bytes 393220
  5.6 17.8 %copy-start.8 = (s32[1,1,1,8]{3,2,1,0:T(1,128)S(1)}, s32[1,1,1,8]{3,2,1,0:T(1,128)}, u32[]{:S(2)}) copy-start(s32[1,1,1,8]{3,2,1,0:T(1,128)} %param.18) | copy-start | bytes 100
  5.8 64.5 %copy-start.7 = (bf16[64,256]{1,0:T(8,128)(2,1)S(1)}, bf16[64,256]{1,0:T(8,128)(2,1)}, u32[]{:S(2)}) copy-start(bf16[64,256]{1,0:T(8,128)(2,1)} %param.19) | copy-start | bytes 98308
  6.5 69.8 %copy-start.11 = (s32[1,1,1,4]{3,2,1,0:T(1,128)S(1)}, s32[1,1,1,4]{3,2,1,0:T(1,128)}, u32[]{:S(2)}) copy-start(s32[1,1,1,4]{3,2,1,0:T(1,128)} %param.12) | copy-start | bytes 52
  6.5 77.5 %all-to-all-start = ((bf16[8,3,16,256]{3,2,1,0:T(8,128)(2,1)}), bf16[8,3,16,256]{3,2,1,0:T(8,128)(2,1)}, u32[]{:S(2)}, u32[]{:S(2)}) async-start(bf16[8,3,16,256]{3,2,1,0:T(8,128)(2,1)} %bitcast.28), calls=%async_computation | async-start | bytes 393216 | tf_op jit(solution)/shard_map/all_to_all | solution.py:89
  14.7 62.3 %collective-permute-start = (bf16[256,256]{1,0:T(8,128)(2,1)S(1)}, bf16[256,256]{1,0:T(8,128)(2,1)S(1)}, u32[]{:S(2)}, u32[]{:S(2)}) collective-permute-start(bf16[256,256]{1,0:T(8,128)(2,1)S(1)} %get-tuple-element.17), channel_id=1, source_target_pairs={{0,16},{1,17},{2,18},{3,19},{4,20},{5,21},{6,22},{7,23},{8,24},{9,... | collective-permute-start | bytes 393224 | tf_op jit(solution)/shard_map/ppermute | solution.py:13
  18.6 60.6 %collective-permute-start.1 = (bf16[256,256]{1,0:T(8,128)(2,1)}, bf16[256,256]{1,0:T(8,128)(2,1)}, u32[]{:S(2)}, u32[]{:S(2)}) collective-permute-start(bf16[256,256]{1,0:T(8,128)(2,1)} %get-tuple-element.16), channel_id=1, source_target_pairs={{16,0},{17,1},{18,2},{19,3},{20,4},{21,5},{22,6},{23,7},{24,8},{25... | collective-permute-start | bytes 393224 | tf_op jit(solution)/shard_map/ppermute | solution.py:13
  19.9 60.9 %collective-permute-start.2 = (bf16[256,256]{1,0:T(8,128)(2,1)}, bf16[256,256]{1,0:T(8,128)(2,1)}, u32[]{:S(2)}, u32[]{:S(2)}) collective-permute-start(bf16[256,256]{1,0:T(8,128)(2,1)} %get-tuple-element.15), channel_id=1, source_target_pairs={{0,4},{4,8},{8,12},{1,5},{5,9},{9,13},{2,6},{6,10},{10,14},{3,7},{... | collective-permute-start | bytes 393224 | tf_op jit(solution)/shard_map/ppermute | solution.py:13
  21.9 60.5 %collective-permute-start.3 = (bf16[256,256]{1,0:T(8,128)(2,1)}, bf16[256,256]{1,0:T(8,128)(2,1)}, u32[]{:S(2)}, u32[]{:S(2)}) collective-permute-start(bf16[256,256]{1,0:T(8,128)(2,1)} %get-tuple-element.14), channel_id=1, source_target_pairs={{4,0},{8,4},{12,8},{5,1},{9,5},{13,9},{6,2},{10,6},{14,10},{7,3},{... | collective-permute-start | bytes 393224 | tf_op jit(solution)/shard_map/ppermute | solution.py:13
  23.7 61.4 %copy-start.1 = (bf16[1,1,1,1536,256]{4,3,2,1,0:T(8,128)(2,1)S(1)}, bf16[1,1,1,1536,256]{4,3,2,1,0:T(8,128)(2,1)}, u32[]{:S(2)}) copy-start(bf16[1,1,1,1536,256]{4,3,2,1,0:T(8,128)(2,1)} %param.10) | copy-start | bytes 2359300
  77.0 0.7 copy-start.6
  89.5 4.8 %copy-start.5 = (bf16[1,1,1,8,1536]{4,3,2,1,0:T(8,128)(2,1)S(1)}, bf16[1,1,1,8,1536]{4,3,2,1,0:T(8,128)(2,1)}, u32[]{:S(2)}) copy-start(bf16[1,1,1,8,1536]{4,3,2,1,0:T(8,128)(2,1)} %param.17) | copy-start | bytes 73732
  99.7 78.5 %all-to-all-start.1 = ((bf16[8,3,16,256]{3,2,1,0:T(8,128)(2,1)}), bf16[8,3,16,256]{3,2,1,0:T(8,128)(2,1)}, u32[]{:S(2)}, u32[]{:S(2)}) async-start(bf16[8,3,16,256]{3,2,1,0:T(8,128)(2,1)} %bitcast.103), calls=%async_computation.1 | async-start | bytes 393216 | tf_op jit(solution)/shard_map/all_to_all | solution.py:89
  105.4 62.9 %collective-permute-start.4 = (bf16[256,256]{1,0:T(8,128)(2,1)}, bf16[256,256]{1,0:T(8,128)(2,1)}, u32[]{:S(2)}, u32[]{:S(2)}) collective-permute-start(bf16[256,256]{1,0:T(8,128)(2,1)} %get-tuple-element.13), channel_id=1, source_target_pairs={{0,16},{1,17},{2,18},{3,19},{4,20},{5,21},{6,22},{7,23},{8,24},{9,... | collective-permute-start | bytes 393224 | tf_op jit(solution)/shard_map/ppermute | solution.py:13
  109.9 60.6 %collective-permute-start.5 = (bf16[256,256]{1,0:T(8,128)(2,1)}, bf16[256,256]{1,0:T(8,128)(2,1)}, u32[]{:S(2)}, u32[]{:S(2)}) collective-permute-start(bf16[256,256]{1,0:T(8,128)(2,1)} %get-tuple-element.12), channel_id=1, source_target_pairs={{16,0},{17,1},{18,2},{19,3},{20,4},{21,5},{22,6},{23,7},{24,8},{25... | collective-permute-start | bytes 393224 | tf_op jit(solution)/shard_map/ppermute | solution.py:13
  111.2 61.6 %collective-permute-start.6 = (bf16[256,256]{1,0:T(8,128)(2,1)}, bf16[256,256]{1,0:T(8,128)(2,1)}, u32[]{:S(2)}, u32[]{:S(2)}) collective-permute-start(bf16[256,256]{1,0:T(8,128)(2,1)} %get-tuple-element.11), channel_id=1, source_target_pairs={{0,4},{4,8},{8,12},{1,5},{5,9},{9,13},{2,6},{6,10},{10,14},{3,7},{... | collective-permute-start | bytes 393224 | tf_op jit(solution)/shard_map/ppermute | solution.py:13
  113.3 61.8 %collective-permute-start.7 = (bf16[256,256]{1,0:T(8,128)(2,1)}, bf16[256,256]{1,0:T(8,128)(2,1)}, u32[]{:S(2)}, u32[]{:S(2)}) collective-permute-start(bf16[256,256]{1,0:T(8,128)(2,1)} %get-tuple-element.10), channel_id=1, source_target_pairs={{4,0},{8,4},{12,8},{5,1},{9,5},{13,9},{6,2},{10,6},{14,10},{7,3},{... | collective-permute-start | bytes 393224 | tf_op jit(solution)/shard_map/ppermute | solution.py:13
  184.3 4.4 %copy-start.2 = (f32[1536,256]{1,0:T(8,128)}, f32[1536,256]{1,0:T(8,128)S(1)}, u32[]{:S(2)}) copy-start(f32[1536,256]{1,0:T(8,128)S(1)} %fusion.6) | copy-start | bytes 4718596
where the time goes:
time: 191 us; the launch traced here: 190 us
  blocking collectives  104 us (54%)
  starting transfers between devices  29.9 us (16%)
  matrix products  27.3 us (14%)
  other arithmetic  17.5 us (9%)
  local copies, waits for them, and re-layouts  9.94 us (5%)
    psum x2, blocking collectives, body(): coarse_sum = lax.psum(partial_sum, ('sx', 'sy', 'sz')).astype(jnp.bfloat16)  92.5 us
    ppermute x8, starting transfers between devices, shifted(): return lax.ppermute(block, axis, route)  17.6 us
    unnamed x8, other arithmetic  15.3 us
    all_to_all x2, starting transfers between devices, body(): lax.all_to_all(outgoing, ('sx', 'sz'), split_axis=0, concat_axis=0, tiled...  12.3 us
    dot_general x3, matrix products, body(): jnp.dot(inverse, multipliers.astype(jnp.bfloat16), preferred_element_type...  12.1 us
    all_gather x2, blocking collectives, body(): coarse_field = lax.all_gather(own_rows, 'sy', axis=0, tiled=True)  11.8 us
    dot_general x2, matrix products, body(): lax.dot_general(patch, arrived.astype(jnp.bfloat16), (((0,), (0,)), ((),...  5.56 us
    dot_general x2, matrix products, body(): lax.dot_general(corners, picked, (((0,), (0,)), ((), ())), preferred_elem...  4.07 us
  transfers between devices with their start and end apart: 10, of which 0 were waited for; matrix products, arithmetic and copies ran while one was open for 11% of the time, Pallas kernels for 0%

commit v1 on v0

v1 whole, which is shorter than its diff:
```python
import functools

import jax
import jax.numpy as jnp
from jax import lax
from jax.experimental import pallas as pl
from jax.experimental.pallas import tpu as pltpu
from jax.sharding import PartitionSpec as P

ITERS = 2
F32 = jnp.float32
BF16 = jnp.bfloat16
MESH = pl.DeviceIdType.MESH


def each(count, step):
    if count <= 16:
        for number in range(count):
            step(number)
    else:

        @pl.loop(0, count)
        def _(number):
            step(number)


def kernel(
    sizes,
    link,
    target,
    rank,
    corner,
    right_hbm,
    inverse_hbm,
    bases_hbm,
    patch_hbm,
    corners_hbm,
    coarse_hbm,
    out_hbm,
    field_hbm,
    right,
    inverse,
    bases,
    patch,
    corners,
    coarse,
    stacked,
    lifted,
    hot,
    mixing,
    rounded,
    solved,
    base,
    face_in,
    tx,
    rx,
    gathered,
    joint,
    final,
    field,
    load_sem,
    store_sem,
    hot_sem,
    coarse_sem,
    face_sem,
    group_sem,
    line_sem,
):
    nx, ny, nz = sizes
    group = nx * nz
    order, columns = right.shape
    face = order // 6
    entries = target.shape[0]
    limit = bases.shape[0] // entries
    count = corner.shape[0]
    twice = 2 * count
    half = columns // 2
    width = coarse.shape[-1]
    i, j, k = (lax.axis_index(name) for name in ("sx", "sy", "sz"))
    me = i * nz + k

    def member(step):
        other = lax.rem(me + 1 + step, group)
        return other // nz, lax.rem(other, nz)

    def in_line(step):
        return lax.rem(j + 1 + step, ny)

    loads = []

    def load(source, place):
        copy = pltpu.make_async_copy(source, place, load_sem.at[len(loads)])
        copy.start()
        loads.append(copy)
        return copy

    load_right = load(right_hbm, right)
    load_rows = [
        load(inverse_hbm.at[pl.ds(f * face, face)], inverse.at[pl.ds(f * face, face)])
        for f in range(6)
    ]
    load_bases = load(bases_hbm, bases)
    load_patch = load(patch_hbm, patch)
    load_corners = load(corners_hbm, corners)
    load_coarse = load(coarse_hbm, coarse.at[j])

    barrier = pltpu.get_barrier_semaphore()

    def greet(step):
        a, c = member(step)
        pl.semaphore_signal(barrier, inc=1, device_id=(a, j, c), device_id_type=MESH)

    def greet_line(step):
        pl.semaphore_signal(barrier, inc=1, device_id=(i, in_line(step), k), device_id_type=MESH)

    each(group - 1, greet)
    each(ny - 1, greet_line)

    row = lax.broadcasted_iota(jnp.int32, (twice, width), 0)
    ids = jnp.zeros((twice, width), jnp.int32)
    for q in range(count):
        ids = jnp.where(lax.rem(row, count) == q, corner[q], ids)
    lane = lax.broadcasted_iota(jnp.int32, (twice, width), 1)
    hot[j, pl.ds(pl.multiple_of(me * twice, twice), twice), :] = jnp.where(
        ids == lane, 1.0, 0.0
    ).astype(BF16)

    for number, axis_index, edge in ((0, i, 0), (1, i, nx - 1), (2, j, 0), (3, j, ny - 1)):

        @pl.when(axis_index == edge)
        def _():
            for sweep in range(ITERS):
                face_in[sweep, number] = jnp.zeros((face, columns), BF16)

    pl.semaphore_wait(barrier, group - 1 + ny - 1)

    own_hot = hot.at[j, pl.ds(pl.multiple_of(me * twice, twice), twice)]

    def send_hot(step):
        a, c = member(step)
        pltpu.make_async_remote_copy(
            own_hot, own_hot, hot_sem.at[0], hot_sem.at[1], device_id=(a, j, c), device_id_type=MESH
        ).start()

    each(group - 1, send_hot)
    load_coarse.wait()

    def send_coarse(step):
        pltpu.make_async_remote_copy(
            coarse.at[j],
            coarse.at[j],
            coarse_sem.at[0],
            coarse_sem.at[1],
            device_id=(i, in_line(step), k),
            device_id_type=MESH,
        ).start()

    each(ny - 1, send_coarse)

    load_bases.wait()
    load_patch.wait()
    load_corners.wait()
    total = entries * limit
    block = min(group * limit, 128)
    lanes = lax.broadcasted_iota(jnp.int32, (1, total), 1)
    entry = lanes // limit
    named = jnp.zeros((1, total), jnp.int32)
    kept = jnp.zeros((1, total), jnp.int32)
    for e in range(entries):
        named = jnp.where(entry == e, target[e], named)
        kept = jnp.where(entry == e, rank[e], kept)
    place = lax.rem(lanes, limit)
    wanted = jnp.where(place < kept, named * limit + place, -1)
    for start in range(0, group * limit, block):
        rows = lax.broadcasted_iota(jnp.int32, (block, total), 0) + start
        route = jnp.where(rows == wanted, 1.0, 0.0).astype(BF16)
        stacked[pl.ds(start, block), :] = jnp.dot(
            route, bases[...], preferred_element_type=F32
        ).astype(BF16)
    padded = jnp.concatenate(
        [corners[...].astype(F32), jnp.zeros((twice - count, order), F32)], axis=0
    )
    stacked[pl.ds(group * limit, twice), :] = padded.astype(BF16)
    lifted[...] = jnp.transpose(
        jnp.concatenate([patch[...].astype(F32), padded], axis=0)
    ).astype(BF16)

    load_right.wait()
    rounded[...] = right[...]

    def face_copy(sweep, f):
        if f < 2:
            to = (i + (1 if f == 1 else -1), j, k)
        else:
            to = (i, j + (1 if f == 3 else -1), k)
        return pltpu.make_async_remote_copy(
            solved.at[sweep, pl.ds(f * face, face)],
            face_in.at[sweep, f ^ 1],
            face_sem.at[sweep, f, 0],
            face_sem.at[sweep, f ^ 1, 1],
            device_id=to,
            device_id_type=MESH,
        )

    def await_face(sweep, f):
        to = ((i - 1, j, k), (i + 1, j, k), (i, j - 1, k), (i, j + 1, k))[f]
        pltpu.make_async_remote_copy(
            solved.at[sweep, pl.ds((f ^ 1) * face, face)],
            face_in.at[sweep, f],
            face_sem.at[sweep, f ^ 1, 0],
            face_sem.at[sweep, f, 1],
            device_id=to,
            device_id_type=MESH,
        ).wait_recv()

    def has(f):
        return (i > 0, i < nx - 1, j > 0, j < ny - 1)[f]

    def send_face(sweep, f):
        @pl.when(has(f))
        def _():
            face_copy(sweep, f).start()

    for sweep in range(ITERS):
        for f in range(6):
            if sweep == 0:
                load_rows[f].wait()
            part = pl.ds(f * face, face)
            product = jnp.dot(
                inverse[part, :], rounded[...], preferred_element_type=F32
            ).astype(BF16)
            solved[sweep, part, :] = product
            if f < 4:
                send_face(sweep, f)

        coefficient = jnp.dot(stacked[...], solved[sweep], preferred_element_type=F32)
        terms = coefficient[group * limit : group * limit + count]
        terms = jnp.concatenate([terms[:, :half], terms[:, half:]], axis=0).astype(BF16)
        for t in range(group):
            own = coefficient[t * limit : (t + 1) * limit].astype(BF16)
            tx[sweep, t, 0:limit, :] = own[:, :half]
            tx[sweep, t, limit : 2 * limit, :] = own[:, half:]
            tx[sweep, t, 2 * limit :, :] = terms

        def send_group(step):
            a, c = member(step)
            pltpu.make_async_remote_copy(
                tx.at[sweep, a * nz + c],
                rx.at[sweep, me],
                group_sem.at[sweep, 0],
                group_sem.at[sweep, 1],
                device_id=(a, j, c),
                device_id_type=MESH,
            ).start()

        each(group - 1, send_group)
        rx[sweep, me] = tx[sweep, me]

        if sweep == 0:
            every = hot.at[j, pl.ds(0, (group - 1) * twice)]
            pltpu.make_async_remote_copy(
                every, every, hot_sem.at[0], hot_sem.at[1], device_id=(i, in_line(0), k),
                device_id_type=MESH,
            ).wait()

            def send_hot_line(step):
                pltpu.make_async_remote_copy(
                    hot.at[j], hot.at[j], hot_sem.at[2], hot_sem.at[3],
                    device_id=(i, in_line(step), k), device_id_type=MESH,
                ).start()

            each(ny - 1, send_hot_line)

        for f in range(6):
            part = pl.ds(f * face, face)
            value = solved[sweep, part, :].astype(F32)
            source = right[part, :].astype(F32)
            before = source if sweep == 0 else final[part, :]
            base[part, :] = before + source - value

        everyone = pltpu.make_async_remote_copy(
            tx.at[sweep, pl.ds(0, group - 1)],
            rx.at[sweep, pl.ds(0, group - 1)],
            group_sem.at[sweep, 0],
            group_sem.at[sweep, 1],
            device_id=(i, in_line(0), k),
            device_id_type=MESH,
        )
        everyone.wait_recv()
        for s in range(group):
            gathered[sweep, j, pl.ds(s * twice, twice), :] = rx[sweep, s, 2 * limit :, :]

        def send_line(step):
            pltpu.make_async_remote_copy(
                gathered.at[sweep, j],
                gathered.at[sweep, j],
                line_sem.at[sweep, 0],
                line_sem.at[sweep, 1],
                device_id=(i, in_line(step), k),
                device_id_type=MESH,
            ).start()

        each(ny - 1, send_line)
        arrived = rx[sweep, 0, 0 : 2 * limit, :].astype(F32)
        for s in range(1, group):
            arrived = arrived + rx[sweep, s, 0 : 2 * limit, :].astype(F32)
        joint[0:limit, :] = jnp.concatenate(
            [arrived[:limit], arrived[limit:]], axis=1
        ).astype(BF16)

        if sweep == 0:
            lines = coarse.at[pl.ds(0, ny - 1)]
            pltpu.make_async_remote_copy(
                lines, lines, coarse_sem.at[0], coarse_sem.at[1],
                device_id=(i, in_line(0), k), device_id_type=MESH,
            ).wait()
            hots = hot.at[pl.ds(0, ny - 1)]
            pltpu.make_async_remote_copy(
                hots, hots, hot_sem.at[2], hot_sem.at[3],
                device_id=(i, in_line(0), k), device_id_type=MESH,
            ).wait()
            picks = jnp.where(ids == lane, 1.0, 0.0).astype(BF16)
            depth = width // ny
            chosen = jnp.zeros((twice, width), F32)
            for y in range(ny):
                chosen = chosen + jnp.dot(
                    picks[:, y * depth : (y + 1) * depth], coarse[y], preferred_element_type=F32
                )
            chosen = chosen.astype(BF16)
            span = group * twice
            upper = lax.broadcasted_iota(jnp.int32, (twice, span), 0) // count
            lower = lax.rem(lax.broadcasted_iota(jnp.int32, (twice, span), 1), twice) // count
            for y in range(ny):
                entries_y = lax.dot_general(
                    chosen, hot[y], (((1,), (1,)), ((), ())), preferred_element_type=F32
                )
                mixing[y] = jnp.where(upper == lower, entries_y, 0.0).astype(BF16)

        pltpu.make_async_remote_copy(
            gathered.at[sweep, pl.ds(0, ny - 1)],
            gathered.at[sweep, pl.ds(0, ny - 1)],
            line_sem.at[sweep, 0],
            line_sem.at[sweep, 1],
            device_id=(i, in_line(0), k),
            device_id_type=MESH,
        ).wait_recv()
        picked = jnp.zeros((twice, half), F32)
        for y in range(ny):
            picked = picked + jnp.dot(mixing[y], gathered[sweep, y], preferred_element_type=F32)
        picked = jnp.concatenate([picked[:count], picked[count:]], axis=1)
        joint[limit:, :] = jnp.concatenate(
            [picked, jnp.zeros((twice - count, columns), F32)], axis=0
        ).astype(BF16)

        for f in (4, 5, 2, 3, 0, 1):
            part = pl.ds(f * face, face)
            if f < 4:

                @pl.when(has(f))
                def _():
                    await_face(sweep, f)

            value = base[part, :] - jnp.dot(
                lifted[part, :], joint[...], preferred_element_type=F32
            )
            if f < 4:
                value = value + link[f].astype(F32) * face_in[sweep, f].astype(F32)
            final[part, :] = value
            rounded[part, :] = value.astype(BF16)
            if sweep == ITERS - 1:
                pltpu.make_async_copy(
                    final.at[part], out_hbm.at[part], store_sem.at[f]
                ).start()

    for f in range(6):
        part = pl.ds(f * face, face)
        field[part, :] = jnp.dot(
            inverse[part, :], rounded[...], preferred_element_type=F32
        ).astype(BF16)
        pltpu.make_async_copy(field.at[part], field_hbm.at[part], store_sem.at[6 + f]).start()

    for sweep in range(ITERS):
        for f in range(4):

            @pl.when(has(f))
            def _():
                face_copy(sweep, f).wait_send()

        pltpu.make_async_remote_copy(
            tx.at[sweep, pl.ds(0, group - 1)],
            rx.at[sweep, pl.ds(0, group - 1)],
            group_sem.at[sweep, 0],
            group_sem.at[sweep, 1],
            device_id=(i, in_line(0), k),
            device_id_type=MESH,
        ).wait_send()
        pltpu.make_async_remote_copy(
            gathered.at[sweep, pl.ds(0, ny - 1)],
            gathered.at[sweep, pl.ds(0, ny - 1)],
            line_sem.at[sweep, 0],
            line_sem.at[sweep, 1],
            device_id=(i, in_line(0), k),
            device_id_type=MESH,
        ).wait_send()
    for f in range(6):
        part = pl.ds(f * face, face)
        pltpu.make_async_copy(final.at[part], out_hbm.at[part], store_sem.at[f]).wait()
        pltpu.make_async_copy(field.at[part], field_hbm.at[part], store_sem.at[6 + f]).wait()


def body(
    right_side,
    interface_inverse,
    face_link,
    far_target,
    far_rank,
    far_basis,
    patch_basis,
    corner_basis,
    corner_row,
    coarse_inverse,
):
    nx, ny, nz = (lax.axis_size(name) for name in ("sx", "sy", "sz"))
    group = nx * nz
    order = interface_inverse.shape[-1]
    columns = right_side.shape[-1]
    face = order // 6
    entries, limit = far_basis.shape[-3:-1]
    count = corner_row.shape[-1]
    depth, width = coarse_inverse.shape
    twice = 2 * count
    half = columns // 2
    stack = group * limit + twice
    message = 2 * limit + twice
    smem = pl.BlockSpec(memory_space=pltpu.SMEM)
    anywhere = pl.BlockSpec(memory_space=pl.ANY)
    multipliers, field = pl.pallas_call(
        functools.partial(kernel, (nx, ny, nz)),
        out_shape=(
            jax.ShapeDtypeStruct((order, columns), F32),
            jax.ShapeDtypeStruct((order, columns), BF16),
        ),
        in_specs=[smem] * 4 + [anywhere] * 6,
        out_specs=(anywhere, anywhere),
        scratch_shapes=[
            pltpu.VMEM((order, columns), BF16),
            pltpu.VMEM((order, order), BF16),
            pltpu.VMEM((entries * limit, order), BF16),
            pltpu.VMEM((limit, order), BF16),
            pltpu.VMEM((count, order), BF16),
            pltpu.VMEM((ny, depth, width), BF16),
            pltpu.VMEM((stack, order), BF16),
            pltpu.VMEM((order, limit + twice), BF16),
            pltpu.VMEM((ny, group * twice, width), BF16),
            pltpu.VMEM((ny, twice, group * twice), BF16),
            pltpu.VMEM((order, columns), BF16),
            pltpu.VMEM((ITERS, order, columns), BF16),
            pltpu.VMEM((order, columns), F32),
            pltpu.VMEM((ITERS, 4, face, columns), BF16),
            pltpu.VMEM((ITERS, group, message, half), BF16),
            pltpu.VMEM((ITERS, group, message, half), BF16),
            pltpu.VMEM((ITERS, ny, group * twice, half), BF16),
            pltpu.VMEM((limit + twice, columns), BF16),
            pltpu.VMEM((order, columns), F32),
            pltpu.VMEM((order, columns), BF16),
            pltpu.SemaphoreType.DMA((11,)),
            pltpu.SemaphoreType.DMA((12,)),
            pltpu.SemaphoreType.DMA((4,)),
            pltpu.SemaphoreType.DMA((2,)),
            pltpu.SemaphoreType.DMA((ITERS, 4, 2)),
            pltpu.SemaphoreType.DMA((ITERS, 2)),
            pltpu.SemaphoreType.DMA((ITERS, 2)),
        ],
        compiler_params=pltpu.CompilerParams(
            collective_id=0, has_side_effects=True, vmem_limit_bytes=60 * 1024 * 1024
        ),
    )(
        face_link.reshape(-1),
        far_target.reshape(-1),
        far_rank.reshape(-1),
        corner_row.reshape(-1),
        right_side.reshape(order, columns),
        interface_inverse.reshape(order, order),
        far_basis.reshape(entries * limit, order),
        patch_basis.reshape(limit, order),
        corner_basis.reshape(count, order),
        coarse_inverse,
    )
    return multipliers.reshape(right_side.shape), field.reshape(right_side.shape)


def solution(mesh):
    wide = P("sx", "sy", "sz", None, None)
    return jax.shard_map(
        body,
        mesh=mesh,
        in_specs=(
            wide,
            wide,
            P("sx", "sy", "sz", None),
            wide,
            P("sx", "sy", "sz", None),
            P("sx", "sy", "sz", None, None, None),
            wide,
            wide,
            P("sx", "sy", "sz", None),
            P("sy", None),
        ),
        out_specs=(wide, wide),
        check_vma=False,
    )
```

time: 191 us -> 37.3 us (0.20)
  blocking collectives: 104 us -> 0 us
  Pallas kernels: 0 us -> 32.9 us
  starting transfers between devices: 29.9 us -> 0 us
  matrix products: 27.3 us -> 0 us
  other arithmetic: 17.5 us -> 0 us
  local copies, waits for them, and re-layouts: 9.94 us -> 3.61 us
    psum x2 -> x0, blocking collectives: 92.5 us -> none  [body(): coarse_sum = lax.psum(partial_sum, ('sx', 'sy', 'sz')).astype(jnp.bfloat16)]
    pallas_call x0 -> x1, Pallas kernels: none -> 32.9 us  [body(): pl.pallas_call(functools.partial(kernel, (nx, ny, nz)), out_shape=(jax.Sh...]
    dot_general x17 -> x0, matrix products: 27.3 us -> none  [the longest x3 12.1 us: body(): jnp.dot(inverse, multipliers.astype(jnp.bfloat16), preferred_element_type...]
    ppermute x8 -> x0, starting transfers between devices: 17.6 us -> none  [shifted(): return lax.ppermute(block, axis, route)]
    unnamed x8 -> x0, other arithmetic: 15.3 us -> none
    all_to_all x2 -> x0, starting transfers between devices: 12.3 us -> none  [body(): lax.all_to_all(outgoing, ('sx', 'sz'), split_axis=0, concat_axis=0, tiled...]
    all_gather x2 -> x0, blocking collectives: 11.8 us -> none  [body(): coarse_field = lax.all_gather(own_rows, 'sy', axis=0, tiled=True)]
    slice x3 -> x0, local copies, waits for them, and re-layouts: 2.23 us -> none  [the longest x2 1.55 us: neighbour_faces(): outgoing = solved[sent_face * face_rows:(sent_face + 1) * face_rows]]
  transfers between devices with their start and end apart: 10 -> 0, of which waited for: 0 -> 0; matrix products, arithmetic and copies ran while one was open for 11% -> 0% of each run, Pallas kernels for 0% -> 0%
where the time goes in v1:
time: 37.3 us; the launch traced here: 37.2 us
  Pallas kernels  32.9 us (88%)
  local copies, waits for them, and re-layouts  3.61 us (10%)
  between operations  0.65 us (2%)
    pallas_call x1, Pallas kernels, body(): pl.pallas_call(functools.partial(kernel, (nx, ny, nz)), out_shape=(jax.Sh...  32.9 us
    unnamed x4, local copies, waits for them, and re-layouts  3.61 us

profile of v1, /device:TPU:0, one launch (start us, length us, event | category | flops | bytes accessed | tf_op | source)
XLA Modules:
  0.0 37.2 jit_solution(2844402704036707778)
XLA Ops:
  0.6 32.9 %shard_map.113 = (f32[1536,256]{1,0:T(8,128)}, bf16[1536,256]{1,0:T(8,128)(2,1)}) custom-call(s32[4]{0:T(128)} %bitcast.18, s32[8]{0:T(128)} %bitcast.19, s32[8]{0:T(128)} %bitcast.20, s32[8]{0:T(128)} %bitcast.21, bf16[1536,256]{1,0:T(8,128)(2,1)} %bitcast.14, bf16[1536,1536]{1,0:T(8,128)(2,1)} %bitcast.11, bf16[128,1536]{1,0:T(8,128)(2,1)} %bitcast.15, ...), custom_call_target="tpu_custom_call" | custom-call | tf_op jit(solution)/shard_map/pallas_call | solution.py:437
  33.6 0.0 copy-start
  33.6 2.7 %copy.14 = f32[1,1,1,1536,256]{4,3,2,1,0:T(8,128)} copy(f32[1,1,1,1536,256]{4,3,2,1,0:T(8,128)} %bitcast.12) | data formatting | bytes 3145728
  36.3 0.0 copy-done
  36.3 0.9 %copy.15 = bf16[1,1,1,1536,256]{4,3,2,1,0:T(8,128)(2,1)} copy(bf16[1,1,1,1536,256]{4,3,2,1,0:T(8,128)(2,1)S(1)} %bitcast.13) | data formatting | bytes 1572864
Async XLA Ops:
  33.6 2.7 %copy-start = (bf16[1536,256]{1,0:T(8,128)(2,1)S(1)}, bf16[1536,256]{1,0:T(8,128)(2,1)}, u32[]{:S(2)}) copy-start(bf16[1536,256]{1,0:T(8,128)(2,1)} %get-tuple-element.5) | copy-start | bytes 2359300

commit v2 on v1

--- a/solution.py
+++ b/solution.py
@@ -37,7 +37,6 @@
     corners_hbm,
     coarse_hbm,
     out_hbm,
-    field_hbm,
     right,
     inverse,
     bases,
@@ -45,7 +44,10 @@
     corners,
     coarse,
     stacked,
+    early,
     lifted,
+    names,
+    every_name,
     hot,
     mixing,
     rounded,
@@ -57,10 +59,9 @@
     gathered,
     joint,
     final,
-    field,
     load_sem,
     store_sem,
-    hot_sem,
+    name_sem,
     coarse_sem,
     face_sem,
     group_sem,
@@ -94,15 +95,15 @@
         loads.append(copy)
         return copy
 
+    load_coarse = load(coarse_hbm, coarse.at[j])
+    load_bases = load(bases_hbm, bases)
+    load_patch = load(patch_hbm, patch)
+    load_corners = load(corners_hbm, corners)
     load_right = load(right_hbm, right)
     load_rows = [
         load(inverse_hbm.at[pl.ds(f * face, face)], inverse.at[pl.ds(f * face, face)])
         for f in range(6)
     ]
-    load_bases = load(bases_hbm, bases)
-    load_patch = load(patch_hbm, patch)
-    load_corners = load(corners_hbm, corners)
-    load_coarse = load(coarse_hbm, coarse.at[j])
 
     barrier = pltpu.get_barrier_semaphore()
 
@@ -116,14 +117,12 @@
     each(group - 1, greet)
     each(ny - 1, greet_line)
 
-    row = lax.broadcasted_iota(jnp.int32, (twice, width), 0)
-    ids = jnp.zeros((twice, width), jnp.int32)
+    row = lax.broadcasted_iota(jnp.int32, names.shape[1:], 0)
+    spot = lax.broadcasted_iota(jnp.int32, names.shape[1:], 1)
+    ids = jnp.zeros(names.shape[1:], jnp.int32)
     for q in range(count):
-        ids = jnp.where(lax.rem(row, count) == q, corner[q], ids)
-    lane = lax.broadcasted_iota(jnp.int32, (twice, width), 1)
-    hot[j, pl.ds(pl.multiple_of(me * twice, twice), twice), :] = jnp.where(
-        ids == lane, 1.0, 0.0
-    ).astype(BF16)
+        ids = jnp.where(row == q, corner[q], ids)
+    names[me] = jnp.where(spot == me, ids, 0).astype(F32)
 
     for number, axis_index, edge in ((0, i, 0), (1, i, nx - 1), (2, j, 0), (3, j, ny - 1)):
 
@@ -131,31 +130,6 @@
         def _():
             for sweep in range(ITERS):
                 face_in[sweep, number] = jnp.zeros((face, columns), BF16)
-
-    pl.semaphore_wait(barrier, group - 1 + ny - 1)
-
-    own_hot = hot.at[j, pl.ds(pl.multiple_of(me * twice, twice), twice)]
-
-    def send_hot(step):
-        a, c = member(step)
-        pltpu.make_async_remote_copy(
-            own_hot, own_hot, hot_sem.at[0], hot_sem.at[1], device_id=(a, j, c), device_id_type=MESH
-        ).start()
-
-    each(group - 1, send_hot)
-    load_coarse.wait()
-
-    def send_coarse(step):
-        pltpu.make_async_remote_copy(
-            coarse.at[j],
-            coarse.at[j],
-            coarse_sem.at[0],
-            coarse_sem.at[1],
-            device_id=(i, in_line(step), k),
-            device_id_type=MESH,
-        ).start()
-
-    each(ny - 1, send_coarse)
 
     load_bases.wait()
     load_patch.wait()
@@ -185,6 +159,30 @@
         jnp.concatenate([patch[...].astype(F32), padded], axis=0)
     ).astype(BF16)
 
+    pl.semaphore_wait(barrier, group - 1 + ny - 1)
+
+    def send_names(step):
+        a, c = member(step)
+        pltpu.make_async_remote_copy(
+            names.at[me], names.at[me], name_sem.at[0], name_sem.at[1],
+            device_id=(a, j, c), device_id_type=MESH,
+        ).start()
+
+    each(group - 1, send_names)
+    load_coarse.wait()
+
+    def send_coarse(step):
+        pltpu.make_async_remote_copy(
+            coarse.at[j],
+            coarse.at[j],
+            coarse_sem.at[0],
+            coarse_sem.at[1],
+            device_id=(i, in_line(step), k),
+            device_id_type=MESH,
+        ).start()
+
+    each(ny - 1, send_coarse)
+
     load_right.wait()
     rounded[...] = right[...]
 
@@ -221,7 +219,32 @@
         def _():
             face_copy(sweep, f).start()
 
+    def pack(sweep, coefficient):
+        terms = coefficient[group * limit : group * limit + count]
+        terms = jnp.concatenate([terms[:, :half], terms[:, half:]], axis=0).astype(BF16)
+        for t in range(group):
+            own = coefficient[t * limit : (t + 1) * limit].astype(BF16)
+            tx[sweep, t, 0:limit, :] = own[:, :half]
+            tx[sweep, t, limit : 2 * limit, :] = own[:, half:]
+            tx[sweep, t, 2 * limit :, :] = terms
+
+        def send_group(step):
+            a, c = member(step)
+            pltpu.make_async_remote_copy(
+                tx.at[sweep, a * nz + c],
+                rx.at[sweep, me],
+                group_sem.at[sweep, 0],
+                group_sem.at[sweep, 1],
+                device_id=(a, j, c),
+                device_id_type=MESH,
+            ).start()
+
+        each(group - 1, send_group)
+        rx[sweep, me] = tx[sweep, me]
+
     for sweep in range(ITERS):
+        if sweep > 0:
+            pack(sweep, jnp.dot(early[...], rounded[...], preferred_element_type=F32))
         for f in range(6):
             if sweep == 0:
                 load_rows[f].wait()
@@ -233,43 +256,22 @@
             if f < 4:
                 send_face(sweep, f)
 
-        coefficient = jnp.dot(stacked[...], solved[sweep], preferred_element_type=F32)
-        terms = coefficient[group * limit : group * limit + count]
-        terms = jnp.concatenate([terms[:, :half], terms[:, half:]], axis=0).astype(BF16)
-        for t in range(group):
-            own = coefficient[t * limit : (t + 1) * limit].astype(BF16)
-            tx[sweep, t, 0:limit, :] = own[:, :half]
-            tx[sweep, t, limit : 2 * limit, :] = own[:, half:]
-            tx[sweep, t, 2 * limit :, :] = terms
-
-        def send_group(step):
-            a, c = member(step)
+        if sweep == 0:
+            pack(sweep, jnp.dot(stacked[...], solved[sweep], preferred_element_type=F32))
+            others = names.at[pl.ds(0, group - 1)]
             pltpu.make_async_remote_copy(
-                tx.at[sweep, a * nz + c],
-                rx.at[sweep, me],
-                group_sem.at[sweep, 0],
-                group_sem.at[sweep, 1],
-                device_id=(a, j, c),
-                device_id_type=MESH,
-            ).start()
-
-        each(group - 1, send_group)
-        rx[sweep, me] = tx[sweep, me]
-
-        if sweep == 0:
-            every = hot.at[j, pl.ds(0, (group - 1) * twice)]
-            pltpu.make_async_remote_copy(
-                every, every, hot_sem.at[0], hot_sem.at[1], device_id=(i, in_line(0), k),
-                device_id_type=MESH,
+                others, others, name_sem.at[0], name_sem.at[1],
+                device_id=(i, in_line(0), k), device_id_type=MESH,
             ).wait()
-
-            def send_hot_line(step):
+            every_name[j] = jnp.sum(names[...], axis=0)
+
+            def send_line_names(step):
                 pltpu.make_async_remote_copy(
-                    hot.at[j], hot.at[j], hot_sem.at[2], hot_sem.at[3],
+                    every_name.at[j], every_name.at[j], name_sem.at[2], name_sem.at[3],
                     device_id=(i, in_line(step), k), device_id_type=MESH,
                 ).start()
 
-            each(ny - 1, send_hot_line)
+            each(ny - 1, send_line_names)
 
         for f in range(6):
             part = pl.ds(f * face, face)
@@ -314,11 +316,22 @@
                 lines, lines, coarse_sem.at[0], coarse_sem.at[1],
                 device_id=(i, in_line(0), k), device_id_type=MESH,
             ).wait()
-            hots = hot.at[pl.ds(0, ny - 1)]
+            lines = every_name.at[pl.ds(0, ny - 1)]
             pltpu.make_async_remote_copy(
-                hots, hots, hot_sem.at[2], hot_sem.at[3],
+                lines, lines, name_sem.at[2], name_sem.at[3],
                 device_id=(i, in_line(0), k), device_id_type=MESH,
             ).wait()
+            for n in range(6):
+                part = pl.ds(n * face, face)
+                early[:, part] = jnp.dot(
+                    stacked[...], inverse[:, part], preferred_element_type=F32
+                ).astype(BF16)
+            row = lax.broadcasted_iota(jnp.int32, (twice, width), 0)
+            lane = lax.broadcasted_iota(jnp.int32, (twice, width), 1)
+            ids = jnp.zeros((twice, width), jnp.int32)
+            for q in range(count):
+                ids = jnp.where(lax.rem(row, count) == q, corner[q], ids)
+            numbers = lax.broadcasted_iota(jnp.int32, (count, width), 1).astype(F32)
             picks = jnp.where(ids == lane, 1.0, 0.0).astype(BF16)
             depth = width // ny
             chosen = jnp.zeros((twice, width), F32)
@@ -331,8 +344,14 @@
             upper = lax.broadcasted_iota(jnp.int32, (twice, span), 0) // count
             lower = lax.rem(lax.broadcasted_iota(jnp.int32, (twice, span), 1), twice) // count
             for y in range(ny):
+                named_y = every_name[y]
+                for s in range(group):
+                    one = jnp.where(named_y[:, s : s + 1] == numbers, 1.0, 0.0)
+                    hot[pl.ds(s * twice, twice), :] = jnp.concatenate(
+                        [one, one], axis=0
+                    ).astype(BF16)
                 entries_y = lax.dot_general(
-                    chosen, hot[y], (((1,), (1,)), ((), ())), preferred_element_type=F32
+                    chosen, hot[...], (((1,), (1,)), ((), ())), preferred_element_type=F32
                 )
                 mixing[y] = jnp.where(upper == lower, entries_y, 0.0).astype(BF16)
 
@@ -372,13 +391,6 @@
                     final.at[part], out_hbm.at[part], store_sem.at[f]
                 ).start()
 
-    for f in range(6):
-        part = pl.ds(f * face, face)
-        field[part, :] = jnp.dot(
-            inverse[part, :], rounded[...], preferred_element_type=F32
-        ).astype(BF16)
-        pltpu.make_async_copy(field.at[part], field_hbm.at[part], store_sem.at[6 + f]).start()
-
     for sweep in range(ITERS):
         for f in range(4):
 
@@ -405,7 +417,33 @@
     for f in range(6):
         part = pl.ds(f * face, face)
         pltpu.make_async_copy(final.at[part], out_hbm.at[part], store_sem.at[f]).wait()
-        pltpu.make_async_copy(field.at[part], field_hbm.at[part], store_sem.at[6 + f]).wait()
+
+
+def last_kernel(inverse_hbm, values_hbm, out_hbm, field_hbm, inverse, values, rounded, field, load_sem, store_sem):
+    face = inverse.shape[0] // 6
+    first = pltpu.make_async_copy(values_hbm, values, load_sem.at[6])
+    first.start()
+    parts = [pl.ds(f * face, face) for f in range(6)]
+    loads = [
+        pltpu.make_async_copy(inverse_hbm.at[part], inverse.at[part], load_sem.at[f])
+        for f, part in enumerate(parts)
+    ]
+    for copy in loads:
+        copy.start()
+    first.wait()
+    stores = [pltpu.make_async_copy(values, out_hbm, store_sem.at[6])]
+    stores[0].start()
+    rounded[...] = values[...].astype(BF16)
+    for f, part in enumerate(parts):
+        loads[f].wait()
+        field[part, :] = jnp.dot(
+            inverse[part, :], rounded[...], preferred_element_type=F32
+        ).astype(BF16)
+        copy = pltpu.make_async_copy(field.at[part], field_hbm.at[part], store_sem.at[f])
+        copy.start()
+        stores.append(copy)
+    for copy in stores:
+        copy.wait()
 
 
 def body(
@@ -432,16 +470,15 @@
     half = columns // 2
     stack = group * limit + twice
     message = 2 * limit + twice
+    lanes = -(-group // 128) * 128
     smem = pl.BlockSpec(memory_space=pltpu.SMEM)
     anywhere = pl.BlockSpec(memory_space=pl.ANY)
-    multipliers, field = pl.pallas_call(
+    matrix = interface_inverse.reshape(order, order)
+    multipliers = pl.pallas_call(
         functools.partial(kernel, (nx, ny, nz)),
-        out_shape=(
-            jax.ShapeDtypeStruct((order, columns), F32),
-            jax.ShapeDtypeStruct((order, columns), BF16),
-        ),
+        out_shape=jax.ShapeDtypeStruct((order, columns), F32),
         in_specs=[smem] * 4 + [anywhere] * 6,
-        out_specs=(anywhere, anywhere),
+        out_specs=anywhere,
         scratch_shapes=[
             pltpu.VMEM((order, columns), BF16),
             pltpu.VMEM((order, order), BF16),
@@ -450,8 +487,11 @@
             pltpu.VMEM((count, order), BF16),
             pltpu.VMEM((ny, depth, width), BF16),
             pltpu.VMEM((stack, order), BF16),
+            pltpu.VMEM((stack, order), BF16),
             pltpu.VMEM((order, limit + twice), BF16),
-            pltpu.VMEM((ny, group * twice, width), BF16),
+            pltpu.VMEM((group, count, lanes), F32),
+            pltpu.VMEM((ny, count, lanes), F32),
+            pltpu.VMEM((group * twice, width), BF16),
             pltpu.VMEM((ny, twice, group * twice), BF16),
             pltpu.VMEM((order, columns), BF16),
             pltpu.VMEM((ITERS, order, columns), BF16),
@@ -462,9 +502,8 @@
             pltpu.VMEM((ITERS, ny, group * twice, half), BF16),
             pltpu.VMEM((limit + twice, columns), BF16),
             pltpu.VMEM((order, columns), F32),
-            pltpu.VMEM((order, columns), BF16),
             pltpu.SemaphoreType.DMA((11,)),
-            pltpu.SemaphoreType.DMA((12,)),
+            pltpu.SemaphoreType.DMA((6,)),
             pltpu.SemaphoreType.DMA((4,)),
             pltpu.SemaphoreType.DMA((2,)),
             pltpu.SemaphoreType.DMA((ITERS, 4, 2)),
@@ -480,12 +519,30 @@
         far_rank.reshape(-1),
         corner_row.reshape(-1),
         right_side.reshape(order, columns),
-        interface_inverse.reshape(order, order),
+        matrix,
         far_basis.reshape(entries * limit, order),
         patch_basis.reshape(limit, order),
         corner_basis.reshape(count, order),
         coarse_inverse,
     )
+    multipliers, field = pl.pallas_call(
+        last_kernel,
+        out_shape=(
+            jax.ShapeDtypeStruct((order, columns), F32),
+            jax.ShapeDtypeStruct((order, columns), BF16),
+        ),
+        in_specs=[anywhere] * 2,
+        out_specs=(anywhere, anywhere),
+        scratch_shapes=[
+            pltpu.VMEM((order, order), BF16),
+            pltpu.VMEM((order, columns), F32),
+            pltpu.VMEM((order, columns), BF16),
+            pltpu.VMEM((order, columns), BF16),
+            pltpu.SemaphoreType.DMA((7,)),
+            pltpu.SemaphoreType.DMA((7,)),
+        ],
+        compiler_params=pltpu.CompilerParams(vmem_limit_bytes=24 * 1024 * 1024),
+    )(matrix, multipliers)
     return multipliers.reshape(right_side.shape), field.reshape(right_side.shape)
 
 

time: 37.3 us -> 37.9 us (1.016)
  Pallas kernels: 32.9 us -> 33.3 us
    pallas_call x1 -> x2, Pallas kernels: 32.9 us -> 33.3 us  [the longest x1 28.7 us: body(): pl.pallas_call(functools.partial(kernel, (nx, ny, nz)), out_shape=jax.Sha...]
where the time goes in v2:
time: 37.9 us; the launch traced here: 37.7 us
  Pallas kernels  33.3 us (88%)
  local copies, waits for them, and re-layouts  3.74 us (10%)
  between operations  0.65 us (2%)
    pallas_call x1, Pallas kernels, body(): pl.pallas_call(functools.partial(kernel, (nx, ny, nz)), out_shape=jax.Sha...  28.7 us
    pallas_call x1, Pallas kernels, body(): pl.pallas_call(last_kernel, out_shape=(jax.ShapeDtypeStruct((order, colum...  4.62 us
    unnamed x4, local copies, waits for them, and re-layouts  3.74 us

profile of v2, /device:TPU:0, one launch (start us, length us, event | category | flops | bytes accessed | tf_op | source)
XLA Modules:
  0.0 37.7 jit_solution(8264149091814934004)
XLA Ops:
  0.6 28.7 %shard_map.113.values_hbm = f32[1536,256]{1,0:T(8,128)} custom-call(s32[4]{0:T(128)} %bitcast.17, s32[8]{0:T(128)} %bitcast.18, s32[8]{0:T(128)} %bitcast.19, s32[8]{0:T(128)} %bitcast.20, bf16[1536,256]{1,0:T(8,128)(2,1)} %bitcast.13, bf16[1536,1536]{1,0:T(8,128)(2,1)} %bitcast.11, bf16[128,1536]{1,0:T(8,128)(2,1)} %bitcast.14, bf16[16,1536]{1,0:T(8,128)(2,1)} %bitcast.15, ...), custom_call_target="tpu_custom_call" | custom-call | tf_op jit(solution)/shard_map/pallas_call | solution.py:477
  29.3 0.0 copy-start
  29.3 2.3 %copy-done = bf16[1,1,1,1536,1536]{4,3,2,1,0:T(8,128)(2,1)S(1)} copy-done((bf16[1,1,1,1536,1536]{4,3,2,1,0:T(8,128)(2,1)S(1)}, bf16[1,1,1,1536,1536]{4,3,2,1,0:T(8,128)(2,1)}, u32[]{:S(2)}) %copy-start) | copy-done | bytes 4718616
  31.6 0.0 copy-start.1
  31.6 1.4 %copy-done.1 = f32[1536,256]{1,0:T(8,128)S(1)} copy-done((f32[1536,256]{1,0:T(8,128)S(1)}, f32[1536,256]{1,0:T(8,128)}, u32[]{:S(2)}) %copy-start.1) | copy-done | bytes 1572888
  33.0 4.6 %shard_map.114 = (f32[1536,256]{1,0:T(8,128)}, bf16[1536,256]{1,0:T(8,128)(2,1)}) custom-call(bf16[1536,1536]{1,0:T(8,128)(2,1)S(1)} %bitcast.12, f32[1536,256]{1,0:T(8,128)S(1)} %copy-done.1), custom_call_target="tpu_custom_call" | custom-call | tf_op jit(solution)/shard_map/pallas_call | solution.py:528
Async XLA Ops:
  29.3 2.3 %copy-start = (bf16[1,1,1,1536,1536]{4,3,2,1,0:T(8,128)(2,1)S(1)}, bf16[1,1,1,1536,1536]{4,3,2,1,0:T(8,128)(2,1)}, u32[]{:S(2)}) copy-start(bf16[1,1,1,1536,1536]{4,3,2,1,0:T(8,128)(2,1)} %param.11) | copy-start | bytes 14155780
  31.6 1.4 %copy-start.1 = (f32[1536,256]{1,0:T(8,128)S(1)}, f32[1536,256]{1,0:T(8,128)}, u32[]{:S(2)}) copy-start(f32[1536,256]{1,0:T(8,128)} %shard_map.113.values_hbm) | copy-start | bytes 4718596

commit v3 on v2

--- a/solution.py
+++ b/solution.py
@@ -36,7 +36,8 @@
     patch_hbm,
     corners_hbm,
     coarse_hbm,
-    out_hbm,
+    final,
+    field,
     right,
     inverse,
     bases,
@@ -58,9 +59,7 @@
     rx,
     gathered,
     joint,
-    final,
     load_sem,
-    store_sem,
     name_sem,
     coarse_sem,
     face_sem,
@@ -242,6 +241,37 @@
         each(group - 1, send_group)
         rx[sweep, me] = tx[sweep, me]
 
+    def forward(sweep):
+        everyone = pltpu.make_async_remote_copy(
+            tx.at[sweep, pl.ds(0, group - 1)],
+            rx.at[sweep, pl.ds(0, group - 1)],
+            group_sem.at[sweep, 0],
+            group_sem.at[sweep, 1],
+            device_id=(i, in_line(0), k),
+            device_id_type=MESH,
+        )
+        everyone.wait_recv()
+        for s in range(group):
+            gathered[sweep, j, pl.ds(s * twice, twice), :] = rx[sweep, s, 2 * limit :, :]
+
+        def send_line(step):
+            pltpu.make_async_remote_copy(
+                gathered.at[sweep, j],
+                gathered.at[sweep, j],
+                line_sem.at[sweep, 0],
+                line_sem.at[sweep, 1],
+                device_id=(i, in_line(step), k),
+                device_id_type=MESH,
+            ).start()
+
+        each(ny - 1, send_line)
+        arrived = rx[sweep, 0, 0 : 2 * limit, :].astype(F32)
+        for s in range(1, group):
+            arrived = arrived + rx[sweep, s, 0 : 2 * limit, :].astype(F32)
+        joint[0:limit, :] = jnp.concatenate(
+            [arrived[:limit], arrived[limit:]], axis=1
+        ).astype(BF16)
+
     for sweep in range(ITERS):
         if sweep > 0:
             pack(sweep, jnp.dot(early[...], rounded[...], preferred_element_type=F32))
@@ -255,6 +285,8 @@
             solved[sweep, part, :] = product
             if f < 4:
                 send_face(sweep, f)
+            if f == 4 and sweep > 0:
+                forward(sweep)
 
         if sweep == 0:
             pack(sweep, jnp.dot(stacked[...], solved[sweep], preferred_element_type=F32))
@@ -280,35 +312,8 @@
             before = source if sweep == 0 else final[part, :]
             base[part, :] = before + source - value
 
-        everyone = pltpu.make_async_remote_copy(
-            tx.at[sweep, pl.ds(0, group - 1)],
-            rx.at[sweep, pl.ds(0, group - 1)],
-            group_sem.at[sweep, 0],
-            group_sem.at[sweep, 1],
-            device_id=(i, in_line(0), k),
-            device_id_type=MESH,
-        )
-        everyone.wait_recv()
-        for s in range(group):
-            gathered[sweep, j, pl.ds(s * twice, twice), :] = rx[sweep, s, 2 * limit :, :]
-
-        def send_line(step):
-            pltpu.make_async_remote_copy(
-                gathered.at[sweep, j],
-                gathered.at[sweep, j],
-                line_sem.at[sweep, 0],
-                line_sem.at[sweep, 1],
-                device_id=(i, in_line(step), k),
-                device_id_type=MESH,
-            ).start()
-
-        each(ny - 1, send_line)
-        arrived = rx[sweep, 0, 0 : 2 * limit, :].astype(F32)
-        for s in range(1, group):
-            arrived = arrived + rx[sweep, s, 0 : 2 * limit, :].astype(F32)
-        joint[0:limit, :] = jnp.concatenate(
-            [arrived[:limit], arrived[limit:]], axis=1
-        ).astype(BF16)
+        if sweep == 0:
+            forward(sweep)
 
         if sweep == 0:
             lines = coarse.at[pl.ds(0, ny - 1)]
@@ -386,10 +391,12 @@
                 value = value + link[f].astype(F32) * face_in[sweep, f].astype(F32)
             final[part, :] = value
             rounded[part, :] = value.astype(BF16)
-            if sweep == ITERS - 1:
-                pltpu.make_async_copy(
-                    final.at[part], out_hbm.at[part], store_sem.at[f]
-                ).start()
+
+    for f in range(6):
+        part = pl.ds(f * face, face)
+        field[part, :] = jnp.dot(
+            inverse[part, :], rounded[...], preferred_element_type=F32
+        ).astype(BF16)
 
     for sweep in range(ITERS):
         for f in range(4):
@@ -414,35 +421,16 @@
             device_id=(i, in_line(0), k),
             device_id_type=MESH,
         ).wait_send()
-    for f in range(6):
-        part = pl.ds(f * face, face)
-        pltpu.make_async_copy(final.at[part], out_hbm.at[part], store_sem.at[f]).wait()
-
-
-def last_kernel(inverse_hbm, values_hbm, out_hbm, field_hbm, inverse, values, rounded, field, load_sem, store_sem):
-    face = inverse.shape[0] // 6
-    first = pltpu.make_async_copy(values_hbm, values, load_sem.at[6])
-    first.start()
-    parts = [pl.ds(f * face, face) for f in range(6)]
-    loads = [
-        pltpu.make_async_copy(inverse_hbm.at[part], inverse.at[part], load_sem.at[f])
-        for f, part in enumerate(parts)
+
+
+def store_kernel(values, field, out_hbm, field_hbm, store_sem):
+    copies = [
+        pltpu.make_async_copy(values, out_hbm, store_sem.at[0]),
+        pltpu.make_async_copy(field, field_hbm, store_sem.at[1]),
     ]
-    for copy in loads:
+    for copy in copies:
         copy.start()
-    first.wait()
-    stores = [pltpu.make_async_copy(values, out_hbm, store_sem.at[6])]
-    stores[0].start()
-    rounded[...] = values[...].astype(BF16)
-    for f, part in enumerate(parts):
-        loads[f].wait()
-        field[part, :] = jnp.dot(
-            inverse[part, :], rounded[...], preferred_element_type=F32
-        ).astype(BF16)
-        copy = pltpu.make_async_copy(field.at[part], field_hbm.at[part], store_sem.at[f])
-        copy.start()
-        stores.append(copy)
-    for copy in stores:
+    for copy in copies:
         copy.wait()
 
 
@@ -472,46 +460,49 @@
     message = 2 * limit + twice
     lanes = -(-group // 128) * 128
     smem = pl.BlockSpec(memory_space=pltpu.SMEM)
-    anywhere = pl.BlockSpec(memory_space=pl.ANY)
-    matrix = interface_inverse.reshape(order, order)
-    multipliers = pl.pallas_call(
+    hbm = pl.BlockSpec(memory_space=pl.ANY)
+    scratch = [
+        pltpu.VMEM((order, columns), BF16),
+        pltpu.VMEM((order, order), BF16),
+        pltpu.VMEM((entries * limit, order), BF16),
+        pltpu.VMEM((limit, order), BF16),
+        pltpu.VMEM((count, order), BF16),
+        pltpu.VMEM((ny, depth, width), BF16),
+        pltpu.VMEM((stack, order), BF16),
+        pltpu.VMEM((stack, order), BF16),
+        pltpu.VMEM((order, limit + twice), BF16),
+        pltpu.VMEM((group, count, lanes), F32),
+        pltpu.VMEM((ny, count, lanes), F32),
+        pltpu.VMEM((group * twice, width), BF16),
+        pltpu.VMEM((ny, twice, group * twice), BF16),
+        pltpu.VMEM((order, columns), BF16),
+        pltpu.VMEM((ITERS, order, columns), BF16),
+        pltpu.VMEM((order, columns), F32),
+        pltpu.VMEM((ITERS, 4, face, columns), BF16),
+        pltpu.VMEM((ITERS, group, message, half), BF16),
+        pltpu.VMEM((ITERS, group, message, half), BF16),
+        pltpu.VMEM((ITERS, ny, group * twice, half), BF16),
+        pltpu.VMEM((limit + twice, columns), BF16),
+        pltpu.SemaphoreType.DMA((11,)),
+        pltpu.SemaphoreType.DMA((4,)),
+        pltpu.SemaphoreType.DMA((2,)),
+        pltpu.SemaphoreType.DMA((ITERS, 4, 2)),
+        pltpu.SemaphoreType.DMA((ITERS, 2)),
+        pltpu.SemaphoreType.DMA((ITERS, 2)),
+    ]
+    vmem = pl.BlockSpec(memory_space=pltpu.VMEM)
+    results = (
+        jax.ShapeDtypeStruct((order, columns), F32),
+        jax.ShapeDtypeStruct((order, columns), BF16),
+    )
+    multipliers, field = pl.pallas_call(
         functools.partial(kernel, (nx, ny, nz)),
-        out_shape=jax.ShapeDtypeStruct((order, columns), F32),
-        in_specs=[smem] * 4 + [anywhere] * 6,
-        out_specs=anywhere,
-        scratch_shapes=[
-            pltpu.VMEM((order, columns), BF16),
-            pltpu.VMEM((order, order), BF16),
-            pltpu.VMEM((entries * limit, order), BF16),
-            pltpu.VMEM((limit, order), BF16),
-            pltpu.VMEM((count, order), BF16),
-            pltpu.VMEM((ny, depth, width), BF16),
-            pltpu.VMEM((stack, order), BF16),
-            pltpu.VMEM((stack, order), BF16),
-            pltpu.VMEM((order, limit + twice), BF16),
-            pltpu.VMEM((group, count, lanes), F32),
-            pltpu.VMEM((ny, count, lanes), F32),
-            pltpu.VMEM((group * twice, width), BF16),
-            pltpu.VMEM((ny, twice, group * twice), BF16),
-            pltpu.VMEM((order, columns), BF16),
-            pltpu.VMEM((ITERS, order, columns), BF16),
-            pltpu.VMEM((order, columns), F32),
-            pltpu.VMEM((ITERS, 4, face, columns), BF16),
-            pltpu.VMEM((ITERS, group, message, half), BF16),
-            pltpu.VMEM((ITERS, group, message, half), BF16),
-            pltpu.VMEM((ITERS, ny, group * twice, half), BF16),
-            pltpu.VMEM((limit + twice, columns), BF16),
-            pltpu.VMEM((order, columns), F32),
-            pltpu.SemaphoreType.DMA((11,)),
-            pltpu.SemaphoreType.DMA((6,)),
-            pltpu.SemaphoreType.DMA((4,)),
-            pltpu.SemaphoreType.DMA((2,)),
-            pltpu.SemaphoreType.DMA((ITERS, 4, 2)),
-            pltpu.SemaphoreType.DMA((ITERS, 2)),
-            pltpu.SemaphoreType.DMA((ITERS, 2)),
-        ],
+        out_shape=results,
+        in_specs=[smem] * 4 + [hbm] * 6,
+        out_specs=(vmem, vmem),
+        scratch_shapes=scratch,
         compiler_params=pltpu.CompilerParams(
-            collective_id=0, has_side_effects=True, vmem_limit_bytes=60 * 1024 * 1024
+            collective_id=0, has_side_effects=True, vmem_limit_bytes=48 * 1024 * 1024
         ),
     )(
         face_link.reshape(-1),
@@ -519,30 +510,19 @@
         far_rank.reshape(-1),
         corner_row.reshape(-1),
         right_side.reshape(order, columns),
-        matrix,
+        interface_inverse.reshape(order, order),
         far_basis.reshape(entries * limit, order),
         patch_basis.reshape(limit, order),
         corner_basis.reshape(count, order),
         coarse_inverse,
     )
     multipliers, field = pl.pallas_call(
-        last_kernel,
-        out_shape=(
-            jax.ShapeDtypeStruct((order, columns), F32),
-            jax.ShapeDtypeStruct((order, columns), BF16),
-        ),
-        in_specs=[anywhere] * 2,
-        out_specs=(anywhere, anywhere),
-        scratch_shapes=[
-            pltpu.VMEM((order, order), BF16),
-            pltpu.VMEM((order, columns), F32),
-            pltpu.VMEM((order, columns), BF16),
-            pltpu.VMEM((order, columns), BF16),
-            pltpu.SemaphoreType.DMA((7,)),
-            pltpu.SemaphoreType.DMA((7,)),
-        ],
-        compiler_params=pltpu.CompilerParams(vmem_limit_bytes=24 * 1024 * 1024),
-    )(matrix, multipliers)
+        store_kernel,
+        out_shape=results,
+        in_specs=[vmem] * 2,
+        out_specs=(hbm, hbm),
+        scratch_shapes=[pltpu.SemaphoreType.DMA((2,))],
+    )(multipliers, field)
     return multipliers.reshape(right_side.shape), field.reshape(right_side.shape)
 
 

time: 37.9 us -> 42.6 us (1.12)
  local copies, waits for them, and re-layouts: 3.74 us -> 9.07 us
  Pallas kernels: 33.3 us -> 32.4 us
    unnamed x4 -> x22, local copies, waits for them, and re-layouts: 3.74 us -> 9.07 us
    pallas_call x2, Pallas kernels: 33.3 us -> 32.4 us  [the longest x1 29.4 us: body(): pl.pallas_call(functools.partial(kernel, (nx, ny, nz)), out_shape=results...]
where the time goes in v3:
time: 42.6 us; the launch traced here: 42.2 us
  Pallas kernels  32.4 us (76%)
  local copies, waits for them, and re-layouts  9.07 us (21%)
  between operations  0.67 us (2%)
    pallas_call x1, Pallas kernels, body(): pl.pallas_call(functools.partial(kernel, (nx, ny, nz)), out_shape=results...  29.4 us
    unnamed x22, local copies, waits for them, and re-layouts  9.07 us
    pallas_call x1, Pallas kernels, body(): pl.pallas_call(store_kernel, out_shape=results, in_specs=[vmem] * 2, out_...  3.02 us

profile of v3, /device:TPU:0, one launch (start us, length us, event | category | flops | bytes accessed | tf_op | source)
XLA Modules:
  0.0 42.2 jit_solution(933890001218728879)
XLA Ops:
  0.6 0.0 copy-start.2
  0.6 1.1 %copy-done.2 = bf16[1,1,1,1536,256]{4,3,2,1,0:T(8,128)(2,1)S(1)} copy-done((bf16[1,1,1,1536,256]{4,3,2,1,0:T(8,128)(2,1)S(1)}, bf16[1,1,1,1536,256]{4,3,2,1,0:T(8,128)(2,1)}, u32[]{:S(2)}) %copy-start.2) | copy-done | bytes 786456
  1.8 0.0 copy-start.3
  1.8 1.0 %copy-done.3 = bf16[1,1,1,8,16,1536]{5,4,3,2,1,0:T(8,128)(2,1)S(1)} copy-done((bf16[1,1,1,8,16,1536]{5,4,3,2,1,0:T(8,128)(2,1)S(1)}, bf16[1,1,1,8,16,1536]{5,4,3,2,1,0:T(8,128)(2,1)}, u32[]{:S(2)}) %copy-start.3) | copy-done | bytes 393240
  2.8 0.0 copy-start.4
  2.8 0.8 %copy-done.4 = bf16[1,1,1,16,1536]{4,3,2,1,0:T(8,128)(2,1)S(1)} copy-done((bf16[1,1,1,16,1536]{4,3,2,1,0:T(8,128)(2,1)S(1)}, bf16[1,1,1,16,1536]{4,3,2,1,0:T(8,128)(2,1)}, u32[]{:S(2)}) %copy-start.4) | copy-done | bytes 49176
  3.6 0.0 copy-start.5
  3.6 0.8 %copy-done.5 = bf16[64,256]{1,0:T(8,128)(2,1)S(1)} copy-done((bf16[64,256]{1,0:T(8,128)(2,1)S(1)}, bf16[64,256]{1,0:T(8,128)(2,1)}, u32[]{:S(2)}) %copy-start.5) | copy-done | bytes 32792
  4.3 0.0 copy-start.6
  4.3 0.7 %copy-done.6 = bf16[1,1,1,8,1536]{4,3,2,1,0:T(8,128)(2,1)S(1)} copy-done((bf16[1,1,1,8,1536]{4,3,2,1,0:T(8,128)(2,1)S(1)}, bf16[1,1,1,8,1536]{4,3,2,1,0:T(8,128)(2,1)}, u32[]{:S(2)}) %copy-start.6) | copy-done | bytes 24600
  5.1 0.0 copy-start.7
  5.1 0.7 %copy-done.7 = s32[1,1,1,4]{3,2,1,0:T(1,128)S(1)} copy-done((s32[1,1,1,4]{3,2,1,0:T(1,128)S(1)}, s32[1,1,1,4]{3,2,1,0:T(1,128)}, u32[]{:S(2)}) %copy-start.7) | copy-done | bytes 40
  5.7 0.0 copy-start.8
  5.7 0.7 %copy-done.8 = s32[1,1,1,8,1]{3,4,2,1,0:T(1,128)S(1)} copy-done((s32[1,1,1,8,1]{3,4,2,1,0:T(1,128)S(1)}, s32[1,1,1,8,1]{3,4,2,1,0:T(1,128)}, u32[]{:S(2)}) %copy-start.8) | copy-done | bytes 56
  6.4 0.0 copy-start.9
  6.4 0.7 %copy-done.9 = s32[1,1,1,8]{3,2,1,0:T(1,128)S(1)} copy-done((s32[1,1,1,8]{3,2,1,0:T(1,128)S(1)}, s32[1,1,1,8]{3,2,1,0:T(1,128)}, u32[]{:S(2)}) %copy-start.9) | copy-done | bytes 56
  7.0 0.0 copy-start.10
  7.0 0.7 %copy-done.10 = s32[1,1,1,8]{3,2,1,0:T(1,128)S(1)} copy-done((s32[1,1,1,8]{3,2,1,0:T(1,128)S(1)}, s32[1,1,1,8]{3,2,1,0:T(1,128)}, u32[]{:S(2)}) %copy-start.10) | copy-done | bytes 56
  7.7 29.4 %shard_map.113 = (f32[1536,256]{1,0:T(8,128)S(1)}, bf16[1536,256]{1,0:T(8,128)(2,1)S(1)}) custom-call(s32[4]{0:T(128)S(1)} %bitcast.15, s32[8]{0:T(128)S(1)} %bitcast.16, s32[8]{0:T(128)S(1)} %bitcast.17, s32[8]{0:T(128)S(1)} %bitcast.18, bf16[1536,256]{1,0:T(8,128)(2,1)S(1)} %bitcast.11, bf16[1536,1536]{1,0:T(8,128)(2,1)} %bitcast.19, ...), custom_call_target="tpu_custom_call" | custom-call | tf_op jit(solution)/shard_map/pallas_call | solution.py:498
  37.1 0.0 copy-start
  37.1 1.2 %copy-done = f32[1536,256]{1,0:T(8,128)} copy-done((f32[1536,256]{1,0:T(8,128)}, f32[1536,256]{1,0:T(8,128)S(1)}, u32[]{:S(2)}) %copy-start) | copy-done | bytes 1572888
  38.3 0.0 copy-start.1
  38.3 0.9 %copy-done.1 = bf16[1536,256]{1,0:T(8,128)(2,1)} copy-done((bf16[1536,256]{1,0:T(8,128)(2,1)}, bf16[1536,256]{1,0:T(8,128)(2,1)S(1)}, u32[]{:S(2)}) %copy-start.1) | copy-done | bytes 786456
  39.2 3.0 %shard_map.114 = (f32[1536,256]{1,0:T(8,128)}, bf16[1536,256]{1,0:T(8,128)(2,1)}) custom-call(f32[1536,256]{1,0:T(8,128)} %copy-done, bf16[1536,256]{1,0:T(8,128)(2,1)} %copy-done.1), custom_call_target="tpu_custom_call" | custom-call | tf_op jit(solution)/shard_map/pallas_call | solution.py:519
Async XLA Ops:
  0.6 1.1 %copy-start.2 = (bf16[1,1,1,1536,256]{4,3,2,1,0:T(8,128)(2,1)S(1)}, bf16[1,1,1,1536,256]{4,3,2,1,0:T(8,128)(2,1)}, u32[]{:S(2)}) copy-start(bf16[1,1,1,1536,256]{4,3,2,1,0:T(8,128)(2,1)} %param.10) | copy-start | bytes 2359300
  1.8 1.0 %copy-start.3 = (bf16[1,1,1,8,16,1536]{5,4,3,2,1,0:T(8,128)(2,1)S(1)}, bf16[1,1,1,8,16,1536]{5,4,3,2,1,0:T(8,128)(2,1)}, u32[]{:S(2)}) copy-start(bf16[1,1,1,8,16,1536]{5,4,3,2,1,0:T(8,128)(2,1)} %param.15) | copy-start | bytes 1179652
  2.8 0.8 %copy-start.4 = (bf16[1,1,1,16,1536]{4,3,2,1,0:T(8,128)(2,1)S(1)}, bf16[1,1,1,16,1536]{4,3,2,1,0:T(8,128)(2,1)}, u32[]{:S(2)}) copy-start(bf16[1,1,1,16,1536]{4,3,2,1,0:T(8,128)(2,1)} %param.16) | copy-start | bytes 147460
  3.6 0.8 %copy-start.5 = (bf16[64,256]{1,0:T(8,128)(2,1)S(1)}, bf16[64,256]{1,0:T(8,128)(2,1)}, u32[]{:S(2)}) copy-start(bf16[64,256]{1,0:T(8,128)(2,1)} %coarse_hbm.1) | copy-start | bytes 98308
  4.3 0.7 %copy-start.6 = (bf16[1,1,1,8,1536]{4,3,2,1,0:T(8,128)(2,1)S(1)}, bf16[1,1,1,8,1536]{4,3,2,1,0:T(8,128)(2,1)}, u32[]{:S(2)}) copy-start(bf16[1,1,1,8,1536]{4,3,2,1,0:T(8,128)(2,1)} %param.17) | copy-start | bytes 73732
  5.1 0.7 %copy-start.7 = (s32[1,1,1,4]{3,2,1,0:T(1,128)S(1)}, s32[1,1,1,4]{3,2,1,0:T(1,128)}, u32[]{:S(2)}) copy-start(s32[1,1,1,4]{3,2,1,0:T(1,128)} %param.12) | copy-start | bytes 52
  5.7 0.7 %copy-start.8 = (s32[1,1,1,8,1]{3,4,2,1,0:T(1,128)S(1)}, s32[1,1,1,8,1]{3,4,2,1,0:T(1,128)}, u32[]{:S(2)}) copy-start(s32[1,1,1,8,1]{3,4,2,1,0:T(1,128)} %param.13) | copy-start | bytes 100
  6.4 0.7 %copy-start.9 = (s32[1,1,1,8]{3,2,1,0:T(1,128)S(1)}, s32[1,1,1,8]{3,2,1,0:T(1,128)}, u32[]{:S(2)}) copy-start(s32[1,1,1,8]{3,2,1,0:T(1,128)} %param.14) | copy-start | bytes 100
  7.0 0.7 %copy-start.10 = (s32[1,1,1,8]{3,2,1,0:T(1,128)S(1)}, s32[1,1,1,8]{3,2,1,0:T(1,128)}, u32[]{:S(2)}) copy-start(s32[1,1,1,8]{3,2,1,0:T(1,128)} %param.18) | copy-start | bytes 100
  37.1 1.2 %copy-start = (f32[1536,256]{1,0:T(8,128)}, f32[1536,256]{1,0:T(8,128)S(1)}, u32[]{:S(2)}) copy-start(f32[1536,256]{1,0:T(8,128)S(1)} %get-tuple-element.6.values) | copy-start | bytes 4718596
  38.3 0.9 %copy-start.1 = (bf16[1536,256]{1,0:T(8,128)(2,1)}, bf16[1536,256]{1,0:T(8,128)(2,1)S(1)}, u32[]{:S(2)}) copy-start(bf16[1536,256]{1,0:T(8,128)(2,1)S(1)} %get-tuple-element.7.field) | copy-start | bytes 2359300

commit v4 on v3

--- a/solution.py
+++ b/solution.py
@@ -36,8 +36,8 @@
     patch_hbm,
     corners_hbm,
     coarse_hbm,
-    final,
-    field,
+    out_hbm,
+    field_hbm,
     right,
     inverse,
     bases,
@@ -59,7 +59,10 @@
     rx,
     gathered,
     joint,
+    final,
+    field,
     load_sem,
+    store_sem,
     name_sem,
     coarse_sem,
     face_sem,
@@ -391,12 +394,17 @@
                 value = value + link[f].astype(F32) * face_in[sweep, f].astype(F32)
             final[part, :] = value
             rounded[part, :] = value.astype(BF16)
+            if sweep == ITERS - 1:
+                pltpu.make_async_copy(
+                    final.at[part], out_hbm.at[part], store_sem.at[f]
+                ).start()
 
     for f in range(6):
         part = pl.ds(f * face, face)
         field[part, :] = jnp.dot(
             inverse[part, :], rounded[...], preferred_element_type=F32
         ).astype(BF16)
+        pltpu.make_async_copy(field.at[part], field_hbm.at[part], store_sem.at[6 + f]).start()
 
     for sweep in range(ITERS):
         for f in range(4):
@@ -421,17 +429,10 @@
             device_id=(i, in_line(0), k),
             device_id_type=MESH,
         ).wait_send()
-
-
-def store_kernel(values, field, out_hbm, field_hbm, store_sem):
-    copies = [
-        pltpu.make_async_copy(values, out_hbm, store_sem.at[0]),
-        pltpu.make_async_copy(field, field_hbm, store_sem.at[1]),
-    ]
-    for copy in copies:
-        copy.start()
-    for copy in copies:
-        copy.wait()
+    for f in range(6):
+        part = pl.ds(f * face, face)
+        pltpu.make_async_copy(final.at[part], out_hbm.at[part], store_sem.at[f]).wait()
+        pltpu.make_async_copy(field.at[part], field_hbm.at[part], store_sem.at[6 + f]).wait()
 
 
 def body(
@@ -483,14 +484,16 @@
         pltpu.VMEM((ITERS, group, message, half), BF16),
         pltpu.VMEM((ITERS, ny, group * twice, half), BF16),
         pltpu.VMEM((limit + twice, columns), BF16),
+        pltpu.VMEM((order, columns), F32),
+        pltpu.VMEM((order, columns), BF16),
         pltpu.SemaphoreType.DMA((11,)),
+        pltpu.SemaphoreType.DMA((12,)),
         pltpu.SemaphoreType.DMA((4,)),
         pltpu.SemaphoreType.DMA((2,)),
         pltpu.SemaphoreType.DMA((ITERS, 4, 2)),
         pltpu.SemaphoreType.DMA((ITERS, 2)),
         pltpu.SemaphoreType.DMA((ITERS, 2)),
     ]
-    vmem = pl.BlockSpec(memory_space=pltpu.VMEM)
     results = (
         jax.ShapeDtypeStruct((order, columns), F32),
         jax.ShapeDtypeStruct((order, columns), BF16),
@@ -499,10 +502,10 @@
         functools.partial(kernel, (nx, ny, nz)),
         out_shape=results,
         in_specs=[smem] * 4 + [hbm] * 6,
-        out_specs=(vmem, vmem),
+        out_specs=(hbm, hbm),
         scratch_shapes=scratch,
         compiler_params=pltpu.CompilerParams(
-            collective_id=0, has_side_effects=True, vmem_limit_bytes=48 * 1024 * 1024
+            collective_id=0, has_side_effects=True, vmem_limit_bytes=60 * 1024 * 1024
         ),
     )(
         face_link.reshape(-1),
@@ -516,13 +519,6 @@
         corner_basis.reshape(count, order),
         coarse_inverse,
     )
-    multipliers, field = pl.pallas_call(
-        store_kernel,
-        out_shape=results,
-        in_specs=[vmem] * 2,
-        out_specs=(hbm, hbm),
-        scratch_shapes=[pltpu.SemaphoreType.DMA((2,))],
-    )(multipliers, field)
     return multipliers.reshape(right_side.shape), field.reshape(right_side.shape)
 
 

time: 42.6 us -> 34.4 us (0.81)
  local copies, waits for them, and re-layouts: 9.07 us -> 3.61 us
  Pallas kernels: 32.4 us -> 30 us
    unnamed x22 -> x4, local copies, waits for them, and re-layouts: 9.07 us -> 3.61 us
    pallas_call x1 -> x0, Pallas kernels: 3.02 us -> none  [body(): pl.pallas_call(store_kernel, out_shape=results, in_specs=[vmem] * 2, out_...]
    pallas_call x1, Pallas kernels: 29.4 us -> 30 us  [body(): pl.pallas_call(functools.partial(kernel, (nx, ny, nz)), out_shape=results...]
where the time goes in v4:
time: 34.4 us; the launch traced here: 34.3 us
  Pallas kernels  30 us (87%)
  local copies, waits for them, and re-layouts  3.61 us (10%)
  between operations  0.65 us (2%)
    pallas_call x1, Pallas kernels, body(): pl.pallas_call(functools.partial(kernel, (nx, ny, nz)), out_shape=results...  30 us
    unnamed x4, local copies, waits for them, and re-layouts  3.61 us

profile of v4, /device:TPU:0, one launch (start us, length us, event | category | flops | bytes accessed | tf_op | source)
XLA Modules:
  0.0 34.3 jit_solution(4297937541513626085)
XLA Ops:
  0.6 30.0 %shard_map.113 = (f32[1536,256]{1,0:T(8,128)}, bf16[1536,256]{1,0:T(8,128)(2,1)}) custom-call(s32[4]{0:T(128)} %bitcast.18, s32[8]{0:T(128)} %bitcast.19, s32[8]{0:T(128)} %bitcast.20, s32[8]{0:T(128)} %bitcast.21, bf16[1536,256]{1,0:T(8,128)(2,1)} %bitcast.14, bf16[1536,1536]{1,0:T(8,128)(2,1)} %bitcast.11, bf16[128,1536]{1,0:T(8,128)(2,1)} %bitcast.15, ...), custom_call_target="tpu_custom_call" | custom-call | tf_op jit(solution)/shard_map/pallas_call | solution.py:501
  30.7 0.0 copy-start
  30.7 2.7 %copy.14 = f32[1,1,1,1536,256]{4,3,2,1,0:T(8,128)} copy(f32[1,1,1,1536,256]{4,3,2,1,0:T(8,128)} %bitcast.12) | data formatting | bytes 3145728
  33.4 0.0 copy-done
  33.4 0.9 %copy.15 = bf16[1,1,1,1536,256]{4,3,2,1,0:T(8,128)(2,1)} copy(bf16[1,1,1,1536,256]{4,3,2,1,0:T(8,128)(2,1)S(1)} %bitcast.13) | data formatting | bytes 1572864
Async XLA Ops:
  30.7 2.7 %copy-start = (bf16[1536,256]{1,0:T(8,128)(2,1)S(1)}, bf16[1536,256]{1,0:T(8,128)(2,1)}, u32[]{:S(2)}) copy-start(bf16[1536,256]{1,0:T(8,128)(2,1)} %get-tuple-element.5) | copy-start | bytes 2359300
